TPU v7x, 32 devices: a whole 2x2x4 slice. The times are simulated.
32 devices in a mesh: band: 8 (over z, x), fld: 4 (over y, core).
Axes of the slice: x: 2, y: 2, z: 4, core: 2. Of those that a mesh axis runs over, the one named last changes fastest.
Arguments:
- grid_fields: bfloat16 [8, 2, 768, 3072], P('fld', None, 'band'), may hold values from -6 to 6
- legendre: bfloat16 [512, 2, 768, 513], P(('band', 'fld')), may hold values from -0.21875 to 0.21875
- slot_wave: int32 [1024], P(('band', 'fld')), may hold values from 0 to 1023, as said below
Outputs:
- spectrum: bfloat16 [512, 2, 8, 2, 513], P(('band', 'fld'))
Inputs may be any that keep to these rules, and one draw needn't show every extreme that they name: `slot_wave`: for every q, slots 2 q and 2 q + 1 hold m and 1023 - m for some m below 512, or both hold 1024; every wavenumber below 1024 is held by exactly one slot.
All inputs are finite; a program needn't handle non-finite values.
Results may differ from a plain program's by a relative error of at most 0.0059.
Values may be sent and summed in bfloat16 or wider, within the bound.
No kernel may reach another device: no remote copies, remote signals or barrier semaphores. Data moves between devices by JAX's collectives and lax.ppermute only.
A program may use at most 64 MiB of HBM per device.

v0:
```python
import math

import jax
import jax.numpy as jnp
from jax import lax
from jax.sharding import PartitionSpec as P

MM = 1024


def slot_table(wave_list, lon_count):
    lon_index = lax.broadcasted_iota(jnp.int32, (lon_count, wave_list.shape[0]), 0)
    phase_index = lon_index * wave_list[None, :] % lon_count
    phase_angle = phase_index.astype(jnp.float32) * (2.0 * math.pi / lon_count)
    norm_scale = 1.0 / math.sqrt(lon_count)
    live_mask = (wave_list < MM)[None, :]
    cosine = jnp.where(live_mask, jnp.cos(phase_angle) * norm_scale, 0.0)
    sine_part = jnp.where(live_mask, -jnp.sin(phase_angle) * norm_scale, 0.0)
    return jnp.stack([cosine, sine_part], axis=1).astype(jnp.bfloat16)


def local(grid_fields, legendre, slot_wave):
    wave_list = lax.all_gather(slot_wave, ("band", "fld"), axis=0, tiled=True)
    fields, hemispheres, lat_rows, lon_count = grid_fields.shape
    slot_count = wave_list.shape[0]
    blocks = max(1, slot_count // 256)
    grid_rows = grid_fields.reshape(fields * hemispheres * lat_rows, lon_count)

    def transform(block_waves):
        fourier_table = slot_table(block_waves, lon_count)
        return jnp.einsum(
            "al,lrs->ars", grid_rows, fourier_table, preferred_element_type=jnp.float32
        )

    blocks_out = lax.map(transform, wave_list.reshape(blocks, -1))
    fourier = jnp.moveaxis(blocks_out, 0, 2).reshape(fields, hemispheres, lat_rows, 2, slot_count)
    north_part = fourier[:, 0]
    south_part = fourier[:, 1]
    folded = jnp.stack([north_part + south_part, north_part - south_part], axis=1).astype(
        jnp.bfloat16
    )
    owner_data = lax.all_to_all(
        lax.all_to_all(folded, "band", split_axis=4, concat_axis=2, tiled=True),
        "fld",
        split_axis=4,
        concat_axis=0,
        tiled=True,
    )
    total_fields, _, half_rows, _, own_slots = owner_data.shape
    pair_count = own_slots // 2
    paired = owner_data.reshape(total_fields, 2, half_rows, 2, pair_count, 2)
    products = jnp.einsum(
        "fphrqk,qphc->qpfrkc", paired, legendre, preferred_element_type=jnp.float32
    )
    own_waves = slot_wave.reshape(pair_count, 2)[:, 0]
    first_wave = own_waves[:, None, None]
    parity = lax.broadcasted_iota(jnp.int32, (1, 2, 1), 1)
    column = lax.broadcasted_iota(jnp.int32, (1, 1, legendre.shape[3]), 2)
    first_count = (MM - first_wave + 1 - parity) // 2
    second_count = (first_wave + 2 - parity) // 2
    first_mask = (column < first_count)[:, :, None, None, :]
    second_mask = ((column >= first_count) & (column < first_count + second_count))[
        :, :, None, None, :
    ]
    spectrum = jnp.where(
        first_mask, products[:, :, :, :, 0], jnp.where(second_mask, products[:, :, :, :, 1], 0.0)
    )
    return spectrum.astype(jnp.bfloat16)


def solution(mesh):
    return jax.shard_map(
        local,
        mesh=mesh,
        in_specs=(
            P("fld", None, "band", None),
            P(("band", "fld"), None, None, None),
            P(("band", "fld")),
        ),
        out_specs=P(("band", "fld"), None, None, None, None),
        check_vma=False,
    )
```

profile of v0, /device:TPU:0, one launch (start us, length us, event | category | flops | bytes accessed | tf_op | source)
XLA Modules:
  0.0 220.2 jit_solution(16350498541361061583)
XLA Ops:
  0.0 0.8 dynamic-update-slice
  0.8 42.0 %all-reduce = s32[1024]{0:T(1024)S(1)} all-reduce(s32[1024]{0:T(1024)S(1)} %dynamic-update-slice), channel_id=1, replica_groups=mesh['band'=8,'fld'=4] {'band','fld'}, use_global_device_ids=true, to_apply=%add | all-reduce | flops 1024 | bytes 8192
  42.8 62.9 %while.12 = (s32[]{:T(128)}, f32[4,384,2,256]{1,3,2,0:T(8,128)S(1)}, s32[4,256]{1,0:T(4,128)S(1)}, bf16[384,3072]{1,0:T(8,128)(2,1)}, s32[]{:T(128)}) while((s32[]{:T(128)}, f32[4,384,2,256]{1,3,2,0:T(8,128)S(1)}, s32[4,256]{1,0:T(4,128)S(1)}, bf16[384,3072]{1,0:T(8,128)(2,1)}, s32[]{:T(128)}) %tuple.39), condition=%wide.region_1.2_spmd, body=%wide.region_0.1_spmd.sunk | while | flops 1222115584 | bytes 18878056 | solution.py:35
  42.8 0.0 copy-start.1
  42.9 13.9 %select_convert_fusion.3 = (bf16[3072,1,256]{0,2,1:T(8,128)(2,1)S(1)}, bf16[3072,1,256]{0,2,1:T(8,128)(2,1)S(1)}) fusion(s32[256]{0:T(256)S(1)} %bitcast.53, pred[256]{0:T(512)(128)(4,1)S(1)} %get-tuple-element.110), kind=kLoop, calls=%fused_computation.8.clone.1 | loop fusion | flops 12582912 | bytes 3147008 | tf_op jit(solution)/shard_map/convert
  56.7 0.0 copy-done.1
  56.8 1.8 fusion.39
  58.6 0.0 copy-start.1
  58.6 13.9 %select_convert_fusion.3 = (bf16[3072,1,256]{0,2,1:T(8,128)(2,1)S(1)}, bf16[3072,1,256]{0,2,1:T(8,128)(2,1)S(1)}) fusion(s32[256]{0:T(256)S(1)} %bitcast.53, pred[256]{0:T(512)(128)(4,1)S(1)} %get-tuple-element.110), kind=kLoop, calls=%fused_computation.8.clone.1 | loop fusion | flops 12582912 | bytes 3147008 | tf_op jit(solution)/shard_map/convert
  72.5 0.0 copy-done.1
  72.5 1.8 fusion.39
  74.3 0.0 copy-start.1
  74.4 13.9 %select_convert_fusion.3 = (bf16[3072,1,256]{0,2,1:T(8,128)(2,1)S(1)}, bf16[3072,1,256]{0,2,1:T(8,128)(2,1)S(1)}) fusion(s32[256]{0:T(256)S(1)} %bitcast.53, pred[256]{0:T(512)(128)(4,1)S(1)} %get-tuple-element.110), kind=kLoop, calls=%fused_computation.8.clone.1 | loop fusion | flops 12582912 | bytes 3147008 | tf_op jit(solution)/shard_map/convert
  88.2 0.0 copy-done.1
  88.2 1.8 fusion.39
  90.1 0.0 copy-start.1
  90.1 13.9 %select_convert_fusion.3 = (bf16[3072,1,256]{0,2,1:T(8,128)(2,1)S(1)}, bf16[3072,1,256]{0,2,1:T(8,128)(2,1)S(1)}) fusion(s32[256]{0:T(256)S(1)} %bitcast.53, pred[256]{0:T(512)(128)(4,1)S(1)} %get-tuple-element.110), kind=kLoop, calls=%fused_computation.8.clone.1 | loop fusion | flops 12582912 | bytes 3147008 | tf_op jit(solution)/shard_map/convert
  104.0 0.0 copy-done.1
  104.0 1.8 fusion.39
  105.8 2.8 %copy.24 = f32[384,2,4,256]{3,2,0,1:T(4,128)} copy(f32[384,2,4,256]{0,3,1,2:T(8,128)S(1)} %bitcast.51) | data formatting | bytes 6291456 | tf_op jit(solution)/shard_map/transpose | solution.py:36
  108.6 3.5 %reshape.342 = f32[2,2,96,2,1024]{4,2,1,0,3:T(8,128)S(1)} reshape(f32[384,2,4,256]{3,2,0,1:T(4,128)} %copy.24) | data formatting | bytes 6291456 | tf_op jit(solution)/shard_map/reshape | solution.py:36
  112.2 0.5 add_convert_fusion
  112.7 1.3 pad_maximum_fusion
  114.0 4.7 %copy.25 = bf16[2,2,96,2,1024]{2,1,0,3,4:T(2,128)(2,1)S(1)} copy(bf16[2,2,96,2,1024]{4,2,1,0,3:T(8,128)(2,1)} %pad_maximum_fusion) | data formatting | bytes 3145728 | tf_op jit(solution)/shard_map/stack | solution.py:39
  118.6 51.7 %all_to_all.33 = bf16[2,2,96,2,1024]{2,1,0,3,4:T(2,128)(2,1)} all-to-all(bf16[2,2,96,2,1024]{2,1,0,3,4:T(2,128)(2,1)S(1)} %copy.25), channel_id=1, replica_groups=mesh['band'=8,'fld'=4] {'band'}, dimensions={4} | all-to-all | bytes 3145728 | tf_op jit(solution)/shard_map/all_to_all | solution.py:43
  170.3 4.8 %copy.37 = bf16[2,2,96,2,8,128]{5,2,4,3,1,0:T(8,128)(2,1)S(1)} copy(bf16[2,2,96,2,8,128]{2,1,0,3,5,4:T(2,128)(2,1)} %bitcast.48) | data formatting | bytes 3145728 | tf_op jit(solution)/shard_map/all_to_all | solution.py:43
  175.1 0.0 copy-start
  175.1 3.0 %copy.28 = bf16[2,2,768,2,128]{2,3,1,0,4:T(2,128)(2,1)} copy(bf16[2,2,768,2,128]{4,2,3,1,0:T(8,128)(2,1)S(1)} %bitcast.49) | data formatting | bytes 3145728 | tf_op jit(solution)/shard_map/all_to_all | solution.py:43
  178.1 3.7 %all-to-all-start.1 = ((bf16[2,2,768,2,128]{2,3,1,0,4:T(2,128)(2,1)}), bf16[2,2,768,2,128]{2,3,1,0,4:T(2,128)(2,1)S(1)}, u32[]{:S(2)}, u32[]{:S(2)}) async-start(bf16[2,2,768,2,128]{2,3,1,0,4:T(2,128)(2,1)} %copy.28), calls=%async_computation.1 | async-start | bytes 3145728 | tf_op jit(solution)/shard_map/all_to_all | solution.py:42
  181.9 0.0 copy-done
  181.9 0.1 reshape.339
  182.0 0.1 subtract_reduce_fusion
  182.1 0.1 add_select_fusion.2
  182.2 0.2 iota_compare_fusion
  182.4 19.4 %all-to-all-done.1 = bf16[2,2,768,2,128]{2,3,1,0,4:T(2,128)(2,1)S(1)} async-done(((bf16[2,2,768,2,128]{2,3,1,0,4:T(2,128)(2,1)}), bf16[2,2,768,2,128]{2,3,1,0,4:T(2,128)(2,1)S(1)}, u32[]{:S(2)}, u32[]{:S(2)}) %all-to-all-start.1) | async-done | bytes 1572896 | tf_op jit(solution)/shard_map/all_to_all | solution.py:42
  201.8 0.3 copy.29
  202.1 1.6 copy.30
  203.7 14.8 %fusion.21 = bf16[16,2,8,2,2,513]{5,2,4,3,1,0:T(8,128)(2,1)S(1)} fusion(bf16[16,2,768,513,1,1]{2,1,3,0,5,4:T(2,128)(2,1)} %bitcast.54, bf16[8,2,768,2,16,2]{2,3,5,4,1,0:T(2,128)(2,1)S(1)} %bitcast.52), kind=kOutput, calls=%fused_computation.19 | convolution fusion | flops 806879232 | bytes 27838464 | tf_op jit(solution)/shard_map/fphrqk,qphc->qpfrkc/dot_general | solution.py:52
  218.5 0.4 fusion.26
  218.8 1.3 copy.34
  (7 shorter events, 0.1 us)
Async XLA Ops:
  42.8 13.9 %copy-start.1 = (bf16[384,3072]{1,0:T(8,128)(2,1)S(1)}, bf16[384,3072]{1,0:T(8,128)(2,1)}, u32[]{:S(2)}) copy-start(bf16[384,3072]{1,0:T(8,128)(2,1)} %get-tuple-element.126) | copy-start | bytes 7077892 | tf_op jit(solution)/shard_map/while
  58.6 13.9 %copy-start.1 = (bf16[384,3072]{1,0:T(8,128)(2,1)S(1)}, bf16[384,3072]{1,0:T(8,128)(2,1)}, u32[]{:S(2)}) copy-start(bf16[384,3072]{1,0:T(8,128)(2,1)} %get-tuple-element.126) | copy-start | bytes 7077892 | tf_op jit(solution)/shard_map/while
  74.3 13.9 %copy-start.1 = (bf16[384,3072]{1,0:T(8,128)(2,1)S(1)}, bf16[384,3072]{1,0:T(8,128)(2,1)}, u32[]{:S(2)}) copy-start(bf16[384,3072]{1,0:T(8,128)(2,1)} %get-tuple-element.126) | copy-start | bytes 7077892 | tf_op jit(solution)/shard_map/while
  90.1 13.9 %copy-start.1 = (bf16[384,3072]{1,0:T(8,128)(2,1)S(1)}, bf16[384,3072]{1,0:T(8,128)(2,1)}, u32[]{:S(2)}) copy-start(bf16[384,3072]{1,0:T(8,128)(2,1)} %get-tuple-element.126) | copy-start | bytes 7077892 | tf_op jit(solution)/shard_map/while
  175.1 6.8 %copy-start = (s32[32]{0:T(128)S(1)}, s32[32]{0:T(128)}, u32[]{:S(2)}) copy-start(s32[32]{0:T(128)} %param.7) | copy-start | bytes 388
  178.1 23.6 %all-to-all-start.1 = ((bf16[2,2,768,2,128]{2,3,1,0,4:T(2,128)(2,1)}), bf16[2,2,768,2,128]{2,3,1,0,4:T(2,128)(2,1)S(1)}, u32[]{:S(2)}, u32[]{:S(2)}) async-start(bf16[2,2,768,2,128]{2,3,1,0,4:T(2,128)(2,1)} %copy.28), calls=%async_computation.1 | async-start | bytes 3145728 | tf_op jit(solution)/shard_map/all_to_all | solution.py:42
where the time goes:
time: 221 us; the launch traced here: 220 us
  blocking collectives  93.7 us (42%)
  other arithmetic  58.1 us (26%)
  local copies, waits for them, and re-layouts  23 us (10%)
  matrix products  22 us (10%)
  waiting for transfers between devices  19.4 us (9%)
  starting transfers between devices  3.74 us (2%)
    another operation x5, other arithmetic  55.9 us
    all_to_all x1, blocking collectives, local(): lax.all_to_all(folded, 'band', split_axis=4, concat_axis=2, tiled=True)  51.7 us
    unnamed x1, blocking collectives  42 us
    all_to_all x1, waiting for transfers between devices, local(): lax.all_to_all(lax.all_to_all(folded, 'band', split_axis=4, concat_axis=2...  19.4 us
    dot_general x1, matrix products, local(): jnp.einsum('fphrqk,qphc->qpfrkc', paired, legendre, preferred_element_typ...  14.8 us
    all_to_all x2, local copies, waits for them, and re-layouts, local(): lax.all_to_all(folded, 'band', split_axis=4, concat_axis=2, tiled=True)  7.78 us
    dot_general x4, matrix products, transform(): jnp.einsum('al,lrs->ars', grid_rows, fourier_table, preferred_element_typ...  7.23 us
    another operation x1, local copies, waits for them, and re-layouts, local(): jnp.stack([north_part + south_part, north_part - south_part], axis=1)  4.66 us
  transfers between devices with their start and end apart: 1, of which 1 were waited for; matrix products, arithmetic and copies ran while one was open for 0% of the time, Pallas kernels for 0%

commit v1 on v0

v1 whole, which is shorter than its diff:
```python
import math

import jax
import jax.numpy as jnp
import numpy as np
from jax import lax
from jax.sharding import PartitionSpec as P

MM = 1024
AXES = ("band", "fld")


def half_table(lon_count):
    index = np.arange(MM // 2)
    even = np.where(index % 2 == 0, index, MM - 1 - index)
    waves = np.stack([even, MM - 1 - even])
    phase = waves[:, :, None] * np.arange(lon_count // 2)[None, None, :] % lon_count
    angle = phase.astype(np.float32) * np.float32(2.0 * math.pi / lon_count)
    scale = 1.0 / math.sqrt(lon_count)
    angle = angle.astype(np.float64)
    table = np.stack([np.cos(angle) * scale, -np.sin(angle) * scale], axis=1)
    return table.astype(np.float32).astype(jnp.bfloat16)


def local(grid_fields, legendre, slot_wave, *, devices):
    fields, _, lat_rows, lon_count = grid_fields.shape
    own_pairs = legendre.shape[0]
    own_waves = slot_wave.reshape(own_pairs, 2)[:, 0]
    wave_list = lax.all_to_all(
        jnp.broadcast_to(own_waves[None], (devices, own_pairs)), AXES, 0, 0, tiled=True
    )
    west = grid_fields[..., : lon_count // 2].astype(jnp.float32)
    east = grid_fields[..., lon_count // 2 :].astype(jnp.float32)
    halves = jnp.stack([west + east, west - east])
    north = halves[:, :, 0]
    south = halves[:, :, 1]
    folded = jnp.stack([north + south, north - south], axis=2).astype(jnp.bfloat16)
    folded = folded.reshape(2, fields * 2 * lat_rows, lon_count // 2)
    table = jnp.asarray(half_table(lon_count))
    fourier = jnp.einsum(
        "eril,eal->iera", table, folded, preferred_element_type=jnp.float32
    ).astype(jnp.bfloat16)
    order = (
        wave_list.reshape(-1)[:, None] == lax.broadcasted_iota(jnp.int32, (1, MM // 2), 1)
    ).astype(jnp.bfloat16)
    sent = jnp.einsum(
        "qi,ix->qx", order, fourier.reshape(MM // 2, -1), preferred_element_type=jnp.float32
    ).astype(jnp.bfloat16)
    got = lax.all_to_all(sent.reshape(devices, own_pairs, -1), AXES, 0, 0, tiled=True)
    bands = legendre.shape[2] // lat_rows
    got = got.reshape(bands, devices // bands, own_pairs, 2, 2, fields, 2, lat_rows)
    data = got.transpose(2, 6, 1, 5, 4, 3, 0, 7).reshape(own_pairs, 2, -1, bands * lat_rows)
    products = jnp.einsum("qpxj,qpjc->qpxc", data, legendre, preferred_element_type=jnp.float32)
    products = products.reshape(own_pairs, 2, -1, 2, 2, legendre.shape[3])
    first_wave = own_waves[:, None, None]
    parity = lax.broadcasted_iota(jnp.int32, (1, 2, 1), 1)
    column = lax.broadcasted_iota(jnp.int32, (1, 1, legendre.shape[3]), 2)
    first_count = (MM - first_wave + 1 - parity) // 2
    second_count = (first_wave + 2 - parity) // 2
    in_first = column < first_count
    live = (column < first_count + second_count) & (first_wave < MM)
    use_even = in_first == (first_wave % 2 == 0)
    spectrum = jnp.where(
        live[:, :, None, None],
        jnp.where(use_even[:, :, None, None], products[..., 0, :], products[..., 1, :]),
        0.0,
    )
    return spectrum.astype(jnp.bfloat16)


def solution(mesh):
    def run(grid_fields, legendre, slot_wave):
        return local(grid_fields, legendre, slot_wave, devices=mesh.size)

    return jax.shard_map(
        run,
        mesh=mesh,
        in_specs=(P("fld", None, "band", None), P(AXES, None, None, None), P(AXES)),
        out_specs=P(AXES, None, None, None, None),
        check_vma=False,
    )
```

time: 221 us -> 95.8 us (0.43)
  blocking collectives: 93.7 us -> 0 us
  other arithmetic: 58.1 us -> 6.69 us
  waiting for transfers between devices: 19.4 us -> 37.3 us
  starting transfers between devices: 3.74 us -> 13.1 us
  local copies, waits for them, and re-layouts: 23 us -> 19.4 us
  matrix products: 22 us -> 18.7 us
    another operation x6 -> x3, other arithmetic: 57.2 us -> 3.21 us  [the longest x1 2.42 us: local(): halves = jnp.stack([west + east, west - east])]
    all_to_all x1 -> x0, blocking collectives: 51.7 us -> none  [local(): lax.all_to_all(folded, 'band', split_axis=4, concat_axis=2, tiled=True)]
    unnamed x1 -> x0, blocking collectives: 42 us -> none
    all_to_all x1 -> x2, waiting for transfers between devices: 19.4 us -> 37.3 us  [the longest x1 37 us: local(): lax.all_to_all(sent.reshape(devices, own_pairs, -1), AXES, 0, 0, tiled=True)]
    reshape x3 -> x5, local copies, waits for them, and re-layouts: 3.63 us -> 14.5 us  [the longest x2 9.65 us: local(): got.reshape(bands, devices // bands, own_pairs, 2, 2, fields, 2, lat_rows)]
    all_to_all x1 -> x2, starting transfers between devices: 3.74 us -> 13.1 us  [the longest x1 7.3 us: local(): lax.all_to_all(jnp.broadcast_to(own_waves[None], (devices, own_pairs)), A...]
    all_to_all x4 -> x1, local copies, waits for them, and re-layouts: 9.69 us -> 0.51 us  [local(): lax.all_to_all(jnp.broadcast_to(own_waves[None], (devices, own_pairs)), A...]
    another operation x1 -> x0, local copies, waits for them, and re-layouts: 4.66 us -> none  [local(): jnp.stack([north_part + south_part, north_part - south_part], axis=1)]
  transfers between devices with their start and end apart: 1 -> 2, of which waited for: 1 -> 2; matrix products, arithmetic and copies ran while one was open for 0% -> 6% of each run, Pallas kernels for 0% -> 0%
where the time goes in v1:
time: 95.8 us; the launch traced here: 95.5 us
  waiting for transfers between devices  37.3 us (39%)
  local copies, waits for them, and re-layouts  19.4 us (20%)
  matrix products  18.7 us (20%)
  starting transfers between devices  13.1 us (14%)
  other arithmetic  6.69 us (7%)
    all_to_all x1, waiting for transfers between devices, local(): lax.all_to_all(sent.reshape(devices, own_pairs, -1), AXES, 0, 0, tiled=True)  37 us
    dot_general x1, matrix products, local(): jnp.einsum('qpxj,qpjc->qpxc', data, legendre, preferred_element_type=jnp....  13.9 us
    reshape x2, local copies, waits for them, and re-layouts, local(): got.reshape(bands, devices // bands, own_pairs, 2, 2, fields, 2, lat_rows)  9.65 us
    all_to_all x1, starting transfers between devices, local(): lax.all_to_all(jnp.broadcast_to(own_waves[None], (devices, own_pairs)), A...  7.3 us
    all_to_all x1, starting transfers between devices, local(): lax.all_to_all(sent.reshape(devices, own_pairs, -1), AXES, 0, 0, tiled=True)  5.84 us
    reshape x1, local copies, waits for them, and re-layouts, local(): got.transpose(2, 6, 1, 5, 4, 3, 0, 7)  3.5 us
    slice x1, local copies, waits for them, and re-layouts, local(): products[..., 0, :]  2.77 us
    dot_general x1, matrix products, local(): jnp.einsum('eril,eal->iera', table, folded, preferred_element_type=jnp.fl...  2.62 us
  transfers between devices with their start and end apart: 2, of which 2 were waited for; matrix products, arithmetic and copies ran while one was open for 6% of the time, Pallas kernels for 0%

profile of v1, /device:TPU:0, one launch (start us, length us, event | category | flops | bytes accessed | tf_op | source)
XLA Modules:
  0.0 95.5 jit_solution(14304612026834837003)
XLA Ops:
  0.0 0.7 reshape.224
  0.7 0.1 slice_reduce_fusion
  0.9 0.6 broadcast_in_dim.29
  1.5 7.3 %all-to-all-start = ((s32[32,1,16]{2,1,0:T(1,128)}), s32[32,1,16]{2,1,0:T(1,128)S(1)}, u32[]{:S(2)}, u32[]{:S(2)}) async-start(s32[32,1,16]{2,1,0:T(1,128)} %broadcast_in_dim.29), calls=%async_computation | async-start | bytes 32768 | tf_op jit(solution)/shard_map/all_to_all | solution.py:29
  8.8 0.0 slice-start
  8.8 2.4 %fusion.2 = (f32[1,2,2,96,1536]{4,3,2,1,0:T(8,128)S(1)}, f32[1,2,2,96,1536]{4,3,2,1,0:T(8,128)S(1)}) fusion(bf16[2,2,96,3072]{3,2,1,0:T(8,128)(2,1)} %param.4), kind=kLoop, calls=%fused_computation.7 | loop fusion | flops 2359296 | bytes 7077888 | tf_op jit(solution)/shard_map/stack | solution.py:34
  11.2 0.0 slice-start.1
  11.2 0.6 add_convert_fusion
  11.8 0.2 pad_maximum_fusion.1
  12.0 0.0 slice-done
  12.1 0.9 slice-done.1
  12.9 2.6 %convolution_convert_fusion.1 = bf16[2,384,2,512]{3,1,2,0:T(8,128)(2,1)S(1)} fusion(bf16[2,384,1536,1]{2,1,3,0:T(8,128)(2,1)S(1)} %bitcast.37, bf16[2,2,512,1536]{3,2,1,0:T(8,128)(2,1)S(1)} %bitcast.39), kind=kOutput, calls=%fused_computation.15 | convolution fusion | flops 2416705536 | bytes 10223616 | tf_op jit(solution)/shard_map/eril,eal->iera/dot_general | solution.py:40
  15.6 0.3 all-to-all-done
  15.9 0.5 broadcast.242
  16.4 0.7 reduce.5
  17.1 0.1 eq.40
  17.1 2.2 %convolution_convert_fusion = bf16[512,1536]{1,0:T(8,128)(2,1)} fusion(bf16[512,1536]{0,1:T(8,128)(2,1)S(1)} %bitcast.40, s32[512]{0:T(512)S(1)} %eq.40), kind=kOutput, calls=%fused_computation.4 | convolution fusion | flops 806354944 | bytes 3147776 | tf_op jit(solution)/shard_map/qi,ix->qx/dot_general | solution.py:46
  19.3 5.8 %all-to-all-start.1 = ((bf16[32,16,1536]{2,1,0:T(8,128)(2,1)}), bf16[32,16,1536]{2,1,0:T(8,128)(2,1)}, u32[]{:S(2)}, u32[]{:S(2)}) async-start(bf16[32,16,1536]{2,1,0:T(8,128)(2,1)} %bitcast.7), calls=%async_computation.1 | async-start | bytes 3145728 | tf_op jit(solution)/shard_map/all_to_all | solution.py:49
  25.2 0.1 fusion.11
  25.3 0.2 compare_compare_fusion
  25.5 37.0 %all-to-all-done.1 = bf16[32,16,1536]{2,1,0:T(8,128)(2,1)} async-done(((bf16[32,16,1536]{2,1,0:T(8,128)(2,1)}), bf16[32,16,1536]{2,1,0:T(8,128)(2,1)}, u32[]{:S(2)}, u32[]{:S(2)}) %all-to-all-start.1) | async-done | bytes 1572896 | tf_op jit(solution)/shard_map/all_to_all | solution.py:49
  62.5 7.0 %reshape.227 = bf16[8,4,16,2,2,2,2,96]{7,6,5,4,3,2,1,0:T(2,128)(2,1)S(1)} reshape(bf16[32,16,1536]{2,1,0:T(8,128)(2,1)} %all-to-all-done.1) | data formatting | bytes 3145728 | tf_op jit(solution)/shard_map/reshape | solution.py:51
  69.5 2.7 %copy.33 = bf16[8,4,16,2,2,2,2,96]{7,0,3,4,5,1,6,2:T(8,128)(2,1)} copy(bf16[8,4,16,2,2,2,2,96]{7,6,5,4,3,2,1,0:T(2,128)(2,1)S(1)} %reshape.227) | data formatting | bytes 3145728 | tf_op jit(solution)/shard_map/reshape | solution.py:51
  72.2 3.5 %reshape.228 = bf16[16,2,32,768]{3,2,1,0:T(8,128)(2,1)S(1)} reshape(bf16[16,2,4,2,2,2,8,96]{7,6,5,4,3,2,1,0:T(8,128)(2,1)} %bitcast.36) | data formatting | bytes 3145728 | tf_op jit(solution)/shard_map/reshape | solution.py:52
  75.7 13.9 %fusion = bf16[16,2,32,513]{3,2,1,0:T(8,128)(2,1)S(1)} fusion(bf16[16,2,32,768]{3,2,1,0:T(8,128)(2,1)S(1)} %reshape.228, bf16[16,2,768,513]{2,1,3,0:T(2,128)(2,1)} %param.5), kind=kOutput, calls=%fused_computation | convolution fusion | flops 806879232 | bytes 27838464 | tf_op jit(solution)/shard_map/qpxj,qpjc->qpxc/dot_general | solution.py:53
  89.6 0.6 reshape.229
  90.2 2.8 %fusion.18 = (bf16[16,2,8,2,1,513]{5,4,3,2,1,0:T(2,128)(2,1)S(1)}, bf16[16,2,8,2,1,513]{5,4,3,2,1,0:T(2,128)(2,1)S(1)}) fusion(bf16[16,2,8,2,2,513]{5,4,3,2,1,0:T(2,128)(2,1)S(1)} %reshape.229), kind=kLoop, calls=%fused_computation.53 | loop fusion | bytes 2101248 | tf_op jit(solution)/shard_map/slice | solution.py:65
  93.0 2.5 %fusion.7 = bf16[16,2,8,2,513]{4,3,2,1,0:T(2,128)(2,1)} fusion(bf16[16,2,8,2,1,513]{5,4,3,2,1,0:T(2,128)(2,1)S(1)} %get-tuple-element.10, bf16[16,2,8,2,1,513]{5,4,3,2,1,0:T(2,128)(2,1)S(1)} %get-tuple-element.9, pred[16,2,513]{2,1,0:T(4,128)(4,1)S(1)} %get-tuple-element.17, pred[16,2,513]{2,1,0:T(4,128)(4,1)S(1)} %get-tuple-element.18), kind=kLoop, calls=%fused_computation.19 | loop fusion | flops 525312 | bytes 1608768 | tf_op jit(solution)/shard_map/convert_element_type | solution.py:68
  (3 shorter events, 0.0 us)
Async XLA Ops:
  1.5 14.4 %all-to-all-start = ((s32[32,1,16]{2,1,0:T(1,128)}), s32[32,1,16]{2,1,0:T(1,128)S(1)}, u32[]{:S(2)}, u32[]{:S(2)}) async-start(s32[32,1,16]{2,1,0:T(1,128)} %broadcast_in_dim.29), calls=%async_computation | async-start | bytes 32768 | tf_op jit(solution)/shard_map/all_to_all | solution.py:29
  8.8 3.3 %slice-start = ((s8[6291456]{0:T(1024)(128)(4,1)}), s8[4194304]{0:T(1024)(128)(4,1)S(1)}, s32[]{:S(2)}) async-start(s8[6291456]{0:T(1024)(128)(4,1)} %bitcast.38), calls=%async_computation.2 | async-start | bytes 8388608
  11.2 1.7 %slice-start.1 = ((s8[6291456]{0:T(1024)(128)(4,1)}), s8[2097152]{0:T(1024)(128)(4,1)S(1)}, s32[]{:S(2)}) async-start(s8[6291456]{0:T(1024)(128)(4,1)} %bitcast.38), calls=%async_computation.3 | async-start | bytes 4194304
  19.3 43.2 %all-to-all-start.1 = ((bf16[32,16,1536]{2,1,0:T(8,128)(2,1)}), bf16[32,16,1536]{2,1,0:T(8,128)(2,1)}, u32[]{:S(2)}, u32[]{:S(2)}) async-start(bf16[32,16,1536]{2,1,0:T(8,128)(2,1)} %bitcast.7), calls=%async_computation.1 | async-start | bytes 3145728 | tf_op jit(solution)/shard_map/all_to_all | solution.py:49

commit v2 on v1

--- a/solution.py
+++ b/solution.py
@@ -1,9 +1,12 @@
+import functools
 import math
 
 import jax
 import jax.numpy as jnp
 import numpy as np
 from jax import lax
+from jax.experimental import pallas as pl
+from jax.experimental.pallas import tpu as pltpu
 from jax.sharding import PartitionSpec as P
 
 MM = 1024
@@ -22,7 +25,7 @@
     return table.astype(np.float32).astype(jnp.bfloat16)
 
 
-def local(grid_fields, legendre, slot_wave, *, devices):
+def general(grid_fields, legendre, slot_wave, *, devices):
     fields, _, lat_rows, lon_count = grid_fields.shape
     own_pairs = legendre.shape[0]
     own_waves = slot_wave.reshape(own_pairs, 2)[:, 0]
@@ -68,14 +71,312 @@
     return spectrum.astype(jnp.bfloat16)
 
 
+NT = (((1,), (1,)), ((), ()))
+GROUP = 4
+AHEAD = 4
+
+
+def repeat_kernel(wave, out):
+    out[...] = jnp.broadcast_to(wave[...], out.shape)
+
+
+def repeated(slot_wave, count):
+    whole = pl.BlockSpec(memory_space=pltpu.VMEM)
+    return pl.pallas_call(
+        repeat_kernel,
+        in_specs=[whole],
+        out_specs=whole,
+        out_shape=jax.ShapeDtypeStruct((count, 1, slot_wave.shape[0]), jnp.int32),
+        name="repeated",
+    )(slot_wave.reshape(1, 1, -1))
+
+
+def transform_kernel(me, grid, table, out, folded):
+    fields, _, rows, lons = grid.shape
+    half = lons // 2
+    turn = (me[0] >> 2) & 3
+    kind = pl.program_id(0)
+
+    for field in range(fields):
+        for row in range(0, rows, 16):
+            part = pl.ds(row, 16)
+            west = [grid[field, side, part, :half].astype(jnp.float32) for side in range(2)]
+            east = [grid[field, side, part, half:].astype(jnp.float32) for side in range(2)]
+            north, south = [
+                jnp.where(kind == 0, west[side] + east[side], west[side] - east[side])
+                for side in range(2)
+            ]
+            for parity in range(2):
+                value = north + south if parity == 0 else north - south
+                place = (field * 2 + parity + turn) & 3
+                at = pl.multiple_of(place * rows + row, 16)
+                folded[pl.ds(at, 16), :] = value.astype(jnp.bfloat16)
+
+    for part in range(2):
+        out[part] = lax.dot_general(
+            table[part], folded[...], NT, preferred_element_type=jnp.float32
+        ).astype(jnp.bfloat16)
+
+
+def transform(me, grid_fields, table):
+    fields, _, rows, lons = grid_fields.shape
+    kinds, waves, half = table.shape
+    lanes = fields * 2 * rows
+    return pl.pallas_call(
+        transform_kernel,
+        grid_spec=pltpu.PrefetchScalarGridSpec(
+            num_scalar_prefetch=1,
+            grid=(2,),
+            in_specs=[
+                pl.BlockSpec(grid_fields.shape, lambda k, me: (0, 0, 0, 0)),
+                pl.BlockSpec((2, waves, half), lambda k, me: (k, 0, 0)),
+            ],
+            out_specs=pl.BlockSpec((2, waves, lanes), lambda k, me: (k, 0, 0)),
+            scratch_shapes=[pltpu.VMEM((lanes, half), jnp.bfloat16)],
+        ),
+        out_shape=jax.ShapeDtypeStruct((kinds, waves, lanes), jnp.bfloat16),
+        compiler_params=pltpu.CompilerParams(vmem_limit_bytes=24 << 20),
+        cost_estimate=pl.CostEstimate(
+            flops=2 * kinds * waves * half * lanes, bytes_accessed=10 << 20, transcendentals=0
+        ),
+        name="transform",
+    )(me, grid_fields, table)
+
+
+def order_kernel(waves, fourier, out, square, picks, rows_f32):
+    kinds, count, lanes = fourier.shape
+    devices, size, _ = out.shape
+    pairs = size // kinds
+    slots = devices * pairs
+    square[...] = jnp.zeros_like(square)
+    for device in range(devices):
+        square[device : device + 1, : 2 * pairs] = waves[device]
+    square[...] = square[...].T
+    number = lax.broadcasted_iota(jnp.int32, (pairs, count), 1)
+    firsts = square[pl.ds(0, pairs, stride=2), :]
+    for device in range(devices):
+        wave = firsts[:, device : device + 1]
+        picks[device * pairs : (device + 1) * pairs, :] = (
+            jnp.where(wave == number, 1.0, 0.0).astype(jnp.bfloat16)
+        )
+    for kind in range(kinds):
+        got = jnp.dot(picks[...], fourier[kind], preferred_element_type=jnp.float32)
+        for tile in range(lanes // 128):
+            rows_f32[tile, pl.ds(kind, slots, stride=kinds), :] = got[:, tile * 128 : tile * 128 + 128]
+    for device in range(devices):
+        for tile in range(lanes // 128):
+            out[device, :, tile * 128 : tile * 128 + 128] = rows_f32[
+                tile, device * size : (device + 1) * size, :
+            ].astype(jnp.bfloat16)
+
+
+def ordered(waves, fourier, pairs):
+    kinds, count, lanes = fourier.shape
+    devices = waves.shape[0]
+    slots = devices * pairs
+    whole = pl.BlockSpec(memory_space=pltpu.VMEM)
+    return pl.pallas_call(
+        order_kernel,
+        in_specs=[whole, whole],
+        out_specs=whole,
+        scratch_shapes=[
+            pltpu.VMEM((128, 128), jnp.int32),
+            pltpu.VMEM((slots, count), jnp.bfloat16),
+            pltpu.VMEM((lanes // 128, kinds * slots, 128), jnp.float32),
+        ],
+        out_shape=jax.ShapeDtypeStruct((devices, kinds * pairs, lanes), jnp.bfloat16),
+        compiler_params=pltpu.CompilerParams(vmem_limit_bytes=24 << 20),
+        cost_estimate=pl.CostEstimate(
+            flops=2 * slots * kinds * count * lanes, bytes_accessed=4 << 20, transcendentals=0
+        ),
+        name="ordered",
+    )(waves, fourier)
+
+
+def turned_kernel(table, out, last):
+    columns, _, lat = table.shape[1:]
+    main = columns - 1
+    out[0] = table[0, :main].reshape(2 * main, lat).T
+    last[0] = table[0, main]
+
+
+def turned(table):
+    pairs, columns, _, lat = table.shape
+    wide = 2 * columns - 2
+    return pl.pallas_call(
+        turned_kernel,
+        grid=(pairs,),
+        in_specs=[pl.BlockSpec((1, columns, 2, lat), lambda i: (i, 0, 0, 0))],
+        out_specs=[
+            pl.BlockSpec((1, lat, wide), lambda i: (i, 0, 0)),
+            pl.BlockSpec((1, 2, lat), lambda i: (i, 0, 0)),
+        ],
+        out_shape=[
+            jax.ShapeDtypeStruct((pairs, lat, wide), jnp.bfloat16),
+            jax.ShapeDtypeStruct((pairs, 2, lat), jnp.bfloat16),
+        ],
+        compiler_params=pltpu.CompilerParams(vmem_limit_bytes=16 << 20),
+        cost_estimate=pl.CostEstimate(
+            flops=20 << 30, bytes_accessed=60 << 20, transcendentals=0
+        ),
+        name="turned",
+    )(table)
+
+
+def legendre_kernel(waves, blocks, table, last, spread, out, held, data, lines, sems):
+    pairs, lat, wide = table.shape
+    lanes = blocks.shape[2]
+    rows = lanes // 4
+    columns = wide // 2 + 1
+    copies = [
+        pltpu.make_async_copy(table.at[pair], held.at[pair], sems.at[pair]) for pair in range(pairs)
+    ]
+    for pair in range(AHEAD):
+        copies[pair].start()
+    lane = lax.broadcasted_iota(jnp.int32, (4 * GROUP, lanes), 1)
+    for group in range(pairs // GROUP):
+        for half in range(2):
+            for field in range(4):
+                have = [
+                    blocks[
+                        (half * 4 + band) * 4 + field, group * 4 * GROUP : (group + 1) * 4 * GROUP, :
+                    ].astype(jnp.float32)
+                    for band in range(4)
+                ]
+                for turn in range(4):
+                    value = have[-turn % 4]
+                    for place in range(1, 4):
+                        value = jnp.where(lane >= place * rows, have[(place - turn) % 4], value)
+                    if turn:
+                        value = pltpu.roll(value, lanes - turn * rows, 1)
+                    line = (field * 2 + turn // 2) * 2
+                    for pair in range(GROUP):
+                        for kind in range(2):
+                            data[
+                                group * GROUP + pair,
+                                turn % 2,
+                                pl.ds(kind * 16 + line, 2),
+                                half * lanes : (half + 1) * lanes,
+                            ] = value[pair * 4 + kind * 2 : pair * 4 + kind * 2 + 2]
+
+    index = lax.broadcasted_iota(jnp.int32, (32, wide), 1)
+    even = index & 1 == 0
+    index = index[:16]
+    parity, column = index & 1, index >> 1
+    for group in range(pairs // GROUP):
+        for pair in range(group * GROUP, (group + 1) * GROUP):
+            copies[pair].wait()
+            if pair + AHEAD < pairs:
+                copies[pair + AHEAD].start()
+            here = data[pair].reshape(64, lat).astype(jnp.bfloat16)
+            both = jnp.dot(here, held[pair], preferred_element_type=jnp.float32)
+            value = jnp.where(even, both[:32], both[32:])
+            wave = waves[pair]
+            first_count = (MM - wave + 1 - parity) >> 1
+            second_count = (wave + 2 - parity) >> 1
+            live = (column < first_count + second_count) & (wave < MM)
+            in_first = jnp.where(column < first_count, 1, 0)
+            value = jnp.where(in_first != (wave & 1), value[:16], value[16:])
+            lines[pair * 16 : pair * 16 + 16, :] = jnp.where(live, value, 0.0).astype(jnp.bfloat16)
+
+        top = group * GROUP * 16
+        for block in range(wide // 256):
+            apart = jnp.dot(
+                lines[top : top + GROUP * 16, block * 256 : block * 256 + 256],
+                spread[...],
+                preferred_element_type=jnp.float32,
+            ).astype(jnp.bfloat16)
+            for pair in range(GROUP):
+                for side in range(2):
+                    piece = apart[pair * 16 : pair * 16 + 16, side * 128 : side * 128 + 128]
+                    out[group * GROUP + pair, side, :, :, block * 128 : block * 128 + 128] = (
+                        piece.reshape(8, 2, 128)
+                    )
+    for pair in range(pairs):
+        wave = waves[pair]
+        for side in range(2):
+            value = jnp.sum(
+                data[pair, side] * last[pair, side : side + 1].astype(jnp.float32), axis=1, keepdims=True
+            )
+            first_count = (MM - wave + 1 - side) >> 1
+            second_count = (wave + 2 - side) >> 1
+            live = (columns - 1 < first_count + second_count) & (wave < MM)
+            in_first = jnp.where(columns - 1 < first_count, 1, 0)
+            value = jnp.where(in_first != (wave & 1), value[:16], value[16:])
+            value = jnp.where(live, value, 0.0).astype(jnp.bfloat16)
+            out[pair, side, :, :, columns - 1 :] = value.reshape(8, 2, 1)
+
+
+def legendre_product(waves, blocks, table, last):
+    pairs, lat, wide = table.shape
+    columns = wide // 2 + 1
+    lane = np.arange(256)
+    spread = np.zeros((256, 256), np.float32)
+    spread[lane, (lane % 2) * 128 + lane // 2] = 1.0
+    whole = pl.BlockSpec(memory_space=pltpu.VMEM)
+    return pl.pallas_call(
+        legendre_kernel,
+        in_specs=[
+            pl.BlockSpec(memory_space=pltpu.SMEM),
+            whole,
+            pl.BlockSpec(memory_space=pl.ANY),
+            whole,
+            whole,
+        ],
+        out_specs=whole,
+        scratch_shapes=[
+            pltpu.VMEM((pairs, lat, wide), jnp.bfloat16),
+            pltpu.VMEM((pairs, 2, 32, lat), jnp.float32),
+            pltpu.VMEM((16 * pairs, wide), jnp.bfloat16),
+            pltpu.SemaphoreType.DMA((pairs,)),
+        ],
+        out_shape=jax.ShapeDtypeStruct((pairs, 2, 8, 2, columns), jnp.bfloat16),
+        compiler_params=pltpu.CompilerParams(vmem_limit_bytes=48 << 20),
+        cost_estimate=pl.CostEstimate(flops=8 << 30, bytes_accessed=30 << 20, transcendentals=0),
+        name="legendre_product",
+    )(waves, blocks, table, last, jnp.asarray(spread.astype(jnp.bfloat16)))
+
+
+def local(grid_fields, legendre, slot_wave, *, devices):
+    lon_count = grid_fields.shape[3]
+    own_pairs = legendre.shape[0]
+    me = lax.axis_index(AXES).astype(jnp.int32).reshape(1)
+    own_waves = slot_wave.reshape(own_pairs, 2)[:, 0]
+    waves = lax.all_to_all(repeated(slot_wave, devices), AXES, 0, 0, tiled=True)
+    table = jnp.asarray(half_table(lon_count).reshape(4, MM // 2, lon_count // 2))
+    fourier = transform(me, HBM(grid_fields), HBM(table))
+    sent = ordered(waves, fourier, own_pairs)
+    got = lax.all_to_all(sent, AXES, 0, 0, tiled=True)
+    rows, last = turned(HBM(legendre.transpose(0, 3, 1, 2)))
+    return legendre_product(own_waves, got, HBM(rows), last)
+
+
+def HBM(array):
+    return pltpu.with_memory_space_constraint(array, pltpu.HBM)
+
+
+def fits(mesh, grid_fields, legendre):
+    fields, _, rows, _ = grid_fields.shape
+    return (
+        mesh.shape["band"] == 8
+        and mesh.shape["fld"] == 4
+        and fields == 8
+        and rows % 128 == 0
+        and rows * 4 // 8 % 128 == 0
+        and legendre.shape[3] % 128 == 1
+        and legendre.shape[0] == MM // 2
+    )
+
+
 def solution(mesh):
     def run(grid_fields, legendre, slot_wave):
-        return local(grid_fields, legendre, slot_wave, devices=mesh.size)
-
-    return jax.shard_map(
-        run,
-        mesh=mesh,
-        in_specs=(P("fld", None, "band", None), P(AXES, None, None, None), P(AXES)),
-        out_specs=P(AXES, None, None, None, None),
-        check_vma=False,
-    )
+        part = local if fits(mesh, grid_fields, legendre) else general
+        return jax.shard_map(
+            functools.partial(part, devices=mesh.size),
+            mesh=mesh,
+            in_specs=(P("fld", None, "band", None), P(AXES, None, None, None), P(AXES)),
+            out_specs=P(AXES, None, None, None, None),
+            check_vma=False,
+        )(grid_fields, legendre, slot_wave)
+
+    return run

time: 95.8 us -> 73.2 us (0.76)
  Pallas kernels: 0 us -> 38.9 us
  waiting for transfers between devices: 37.3 us -> 12.8 us
  matrix products: 18.7 us -> 0 us
  local copies, waits for them, and re-layouts: 19.4 us -> 8.5 us
  other arithmetic: 6.69 us -> 0 us
    pallas_call x0 -> x5, Pallas kernels: none -> 38.9 us  [the longest x1 16.7 us: turned(): pl.pallas_call(turned_kernel, grid=(pairs,), in_specs=[pl.BlockSpec((1, c...]
    all_to_all x2, waiting for transfers between devices: 37.3 us -> 12.8 us  [the longest x1 12.2 us: local(): got = lax.all_to_all(sent, AXES, 0, 0, tiled=True)]
    dot_general x3 -> x0, matrix products: 18.7 us -> none  [the longest x1 13.9 us: local(): jnp.einsum('qpxj,qpjc->qpxc', data, legendre, preferred_element_type=jnp....]
    reshape x4 -> x0, local copies, waits for them, and re-layouts: 13.7 us -> none  [the longest x2 9.65 us: local(): got.reshape(bands, devices // bands, own_pairs, 2, 2, fields, 2, lat_rows)]
    unnamed x4 -> x6, local copies, waits for them, and re-layouts: 0.89 us -> 8.31 us
    another operation x3 -> x0, other arithmetic: 3.21 us -> none  [the longest x1 2.42 us: local(): halves = jnp.stack([west + east, west - east])]
    slice x1 -> x0, local copies, waits for them, and re-layouts: 2.77 us -> none  [local(): products[..., 0, :]]
    convert_element_type x1 -> x0, other arithmetic: 2.5 us -> none  [local(): return spectrum.astype(jnp.bfloat16)]
  transfers between devices with their start and end apart: 2 -> 2, of which waited for: 2 -> 2; matrix products, arithmetic and copies ran while one was open for 6% -> 0% of each run, Pallas kernels for 0% -> 32%
where the time goes in v2:
time: 73.2 us; the launch traced here: 72.8 us
  Pallas kernels  38.9 us (53%)
  waiting for transfers between devices  12.8 us (17%)
  starting transfers between devices  12.5 us (17%)
  local copies, waits for them, and re-layouts  8.5 us (12%)
    pallas_call x1, Pallas kernels, turned(): pl.pallas_call(turned_kernel, grid=(pairs,), in_specs=[pl.BlockSpec((1, c...  16.7 us
    all_to_all x1, waiting for transfers between devices, local(): got = lax.all_to_all(sent, AXES, 0, 0, tiled=True)  12.2 us
    pallas_call x1, Pallas kernels, legendre_product(): pl.pallas_call(legendre_kernel, in_specs=[pl.BlockSpec(memory_space=pltpu...  11.5 us
    unnamed x6, local copies, waits for them, and re-layouts  8.31 us
    all_to_all x1, starting transfers between devices, local(): waves = lax.all_to_all(repeated(slot_wave, devices), AXES, 0, 0, tiled=True)  7.3 us
    pallas_call x1, Pallas kernels, transform(): pl.pallas_call(transform_kernel, grid_spec=pltpu.PrefetchScalarGridSpec(n...  6.5 us
    all_to_all x1, starting transfers between devices, local(): got = lax.all_to_all(sent, AXES, 0, 0, tiled=True)  5.24 us
    pallas_call x1, Pallas kernels, ordered(): pl.pallas_call(order_kernel, in_specs=[whole, whole], out_specs=whole, sc...  2.84 us
  transfers between devices with their start and end apart: 2, of which 2 were waited for; matrix products, arithmetic and copies ran while one was open for 0% of the time, Pallas kernels for 32%

profile of v2, /device:TPU:0, one launch (start us, length us, event | category | flops | bytes accessed | tf_op | source)
XLA Modules:
  0.0 72.8 jit_solution(1865320655260321656)
XLA Ops:
  0.0 1.3 %repeated.1 = s32[32,1,32]{2,1,0:T(1,128)} custom-call(s32[1,1,32]{2,1,0:T(1,128)} %bitcast.3), custom_call_target="tpu_custom_call" | custom-call | tf_op jit(solution)/shard_map/repeated/pallas_call | solution.py:85
  1.3 7.3 %all-to-all-start = ((s32[32,1,32]{2,1,0:T(1,128)}), s32[32,1,32]{2,1,0:T(1,128)S(1)}, u32[]{:S(2)}, u32[]{:S(2)}) async-start(s32[32,1,32]{2,1,0:T(1,128)} %repeated.1), calls=%async_computation | async-start | bytes 32768 | tf_op jit(solution)/shard_map/all_to_all | solution.py:345
  8.6 6.5 %transform.1.fourier = bf16[4,512,384]{2,1,0:T(8,128)(2,1)S(1)} custom-call(s32[1]{0:T(128)} %bitcast.1.me, bf16[2,2,96,3072]{3,2,1,0:T(8,128)(2,1)} %grid.1, bf16[4,512,1536]{2,1,0:T(8,128)(2,1)} %constant.15.clone.table), custom_call_target="tpu_custom_call" | custom-call | flops 2415919104 | bytes 10485760 | tf_op jit(solution)/shard_map/transform/pallas_call | solution.py:125
  15.1 0.6 all-to-all-done.waves
  15.6 2.8 %ordered.1 = bf16[32,64,384]{2,1,0:T(8,128)(2,1)} custom-call(s32[32,1,32]{2,1,0:T(1,128)S(1)} %all-to-all-done.waves, bf16[4,512,384]{2,1,0:T(8,128)(2,1)S(1)} %transform.1.fourier), custom_call_target="tpu_custom_call" | custom-call | flops 805306368 | bytes 4194304 | tf_op jit(solution)/shard_map/ordered/pallas_call | solution.py:178
  18.5 0.0 copy-start.2
  18.5 5.2 %all-to-all-start.1 = ((bf16[32,64,384]{2,1,0:T(8,128)(2,1)}), bf16[32,64,384]{2,1,0:T(8,128)(2,1)S(1)}, u32[]{:S(2)}, u32[]{:S(2)}) async-start(bf16[32,64,384]{2,1,0:T(8,128)(2,1)} %ordered.1), calls=%async_computation.1 | async-start | bytes 3145728 | tf_op jit(solution)/shard_map/all_to_all | solution.py:349
  23.7 0.0 copy-done.2
  23.7 0.1 reshape.9
  23.8 0.1 slice_reduce_fusion.waves
  23.9 0.0 copy-start
  24.0 16.7 %turned.1 = (bf16[16,768,1024]{2,1,0:T(8,128)(2,1)S(1)}, bf16[16,2,768]{2,1,0:T(2,128)(2,1)S(1)}) custom-call(bf16[16,513,2,768]{3,2,1,0:T(2,128)(2,1)} %bitcast.4), custom_call_target="tpu_custom_call" | custom-call | flops 21474836480 | bytes 62914560 | tf_op jit(solution)/shard_map/turned/pallas_call | solution.py:206
  40.7 0.0 copy-start.1
  40.7 8.3 %copy-done.1 = bf16[16,768,1024]{2,1,0:T(8,128)(2,1)} copy-done((bf16[16,768,1024]{2,1,0:T(8,128)(2,1)}, bf16[16,768,1024]{2,1,0:T(8,128)(2,1)S(1)}, u32[]{:S(2)}) %copy-start.1) | copy-done | bytes 25165848
  49.0 12.2 %all-to-all-done.1.blocks = bf16[32,64,384]{2,1,0:T(8,128)(2,1)S(1)} async-done(((bf16[32,64,384]{2,1,0:T(8,128)(2,1)}), bf16[32,64,384]{2,1,0:T(8,128)(2,1)S(1)}, u32[]{:S(2)}, u32[]{:S(2)}) %all-to-all-start.1) | async-done | bytes 1572896 | tf_op jit(solution)/shard_map/all_to_all | solution.py:349
  61.2 0.0 copy-done
  61.2 11.5 %legendre_product.1 = bf16[16,2,8,2,513]{4,3,2,1,0:T(2,128)(2,1)} custom-call(s32[16]{0:T(128)S(1)} %slice_reduce_fusion.waves, bf16[32,64,384]{2,1,0:T(8,128)(2,1)S(1)} %all-to-all-done.1.blocks, bf16[16,768,1024]{2,1,0:T(8,128)(2,1)} %copy-done.1, bf16[16,2,768]{2,1,0:T(2,128)(2,1)S(1)} %get-tuple-element.8.last, bf16[256,256]{1,0:T(8,128)(2,1)S(1)} %copy-done), custom_call_target="tpu_custom_call" | custom-call | flops 8589934592 | bytes 31457280 | tf_op jit(solution)/shard_map/legendre_product/pallas_call | solution.py:317
Async XLA Ops:
  1.3 14.4 %all-to-all-start = ((s32[32,1,32]{2,1,0:T(1,128)}), s32[32,1,32]{2,1,0:T(1,128)S(1)}, u32[]{:S(2)}, u32[]{:S(2)}) async-start(s32[32,1,32]{2,1,0:T(1,128)} %repeated.1), calls=%async_computation | async-start | bytes 32768 | tf_op jit(solution)/shard_map/all_to_all | solution.py:345
  18.5 5.2 %copy-start.2 = (s32[32]{0:T(128)S(1)}, s32[32]{0:T(128)}, u32[]{:S(2)}) copy-start(s32[32]{0:T(128)} %param.7) | copy-start | bytes 388
  18.5 42.8 %all-to-all-start.1 = ((bf16[32,64,384]{2,1,0:T(8,128)(2,1)}), bf16[32,64,384]{2,1,0:T(8,128)(2,1)S(1)}, u32[]{:S(2)}, u32[]{:S(2)}) async-start(bf16[32,64,384]{2,1,0:T(8,128)(2,1)} %ordered.1), calls=%async_computation.1 | async-start | bytes 3145728 | tf_op jit(solution)/shard_map/all_to_all | solution.py:349
  23.9 37.3 %copy-start = (bf16[256,256]{1,0:T(8,128)(2,1)S(1)}, bf16[256,256]{1,0:T(8,128)(2,1)}, u32[]{:S(2)}) copy-start(bf16[256,256]{1,0:T(8,128)(2,1)} %constant.16.clone.spread) | copy-start | bytes 393220
  40.7 8.3 %copy-start.1 = (bf16[16,768,1024]{2,1,0:T(8,128)(2,1)}, bf16[16,768,1024]{2,1,0:T(8,128)(2,1)S(1)}, u32[]{:S(2)}) copy-start(bf16[16,768,1024]{2,1,0:T(8,128)(2,1)S(1)} %get-tuple-element.7.table) | copy-start | bytes 75497472

commit v3 on v2

--- a/solution.py
+++ b/solution.py
@@ -13,8 +13,7 @@
 AXES = ("band", "fld")
 
 
-def half_table(lon_count):
-    index = np.arange(MM // 2)
+def half_table(lon_count, index):
     even = np.where(index % 2 == 0, index, MM - 1 - index)
     waves = np.stack([even, MM - 1 - even])
     phase = waves[:, :, None] * np.arange(lon_count // 2)[None, None, :] % lon_count
@@ -39,7 +38,7 @@
     south = halves[:, :, 1]
     folded = jnp.stack([north + south, north - south], axis=2).astype(jnp.bfloat16)
     folded = folded.reshape(2, fields * 2 * lat_rows, lon_count // 2)
-    table = jnp.asarray(half_table(lon_count))
+    table = jnp.asarray(half_table(lon_count, np.arange(MM // 2)))
     fourier = jnp.einsum(
         "eril,eal->iera", table, folded, preferred_element_type=jnp.float32
     ).astype(jnp.bfloat16)
@@ -73,7 +72,7 @@
 
 NT = (((1,), (1,)), ((), ()))
 GROUP = 4
-AHEAD = 4
+AHEAD = 16
 
 
 def repeat_kernel(wave, out):
@@ -91,59 +90,108 @@
     )(slot_wave.reshape(1, 1, -1))
 
 
-def transform_kernel(me, grid, table, out, folded):
-    fields, _, rows, lons = grid.shape
+def quarter_order(row):
+    low = 4 * ((row % (MM // 4)) // 2)
+    return low + (row // (MM // 4)) + (row % 2) * (3 - 2 * (row // (MM // 4)))
+
+
+def transform_kernel(me, grid, table, out, grid_here, table_here, folded, grid_sems, table_sems):
+    fields, _, rows, lons = grid_here.shape
     half = lons // 2
+    quarter = half // 2
     turn = (me[0] >> 2) & 3
-    kind = pl.program_id(0)
-
-    for field in range(fields):
+    grid_copies = [
+        pltpu.make_async_copy(grid.at[field], grid_here.at[field], grid_sems.at[field])
+        for field in range(fields)
+    ]
+    table_copies = [
+        pltpu.make_async_copy(table.at[part], table_here.at[part], table_sems.at[part])
+        for part in range(table.shape[0])
+    ]
+    for copy in grid_copies + table_copies:
+        copy.start()
+
+    def fold(kind, field):
         for row in range(0, rows, 16):
             part = pl.ds(row, 16)
-            west = [grid[field, side, part, :half].astype(jnp.float32) for side in range(2)]
-            east = [grid[field, side, part, half:].astype(jnp.float32) for side in range(2)]
+            west = [grid_here[field, side, part, :half].astype(jnp.float32) for side in range(2)]
+            east = [grid_here[field, side, part, half:].astype(jnp.float32) for side in range(2)]
             north, south = [
-                jnp.where(kind == 0, west[side] + east[side], west[side] - east[side])
+                west[side] + east[side] if kind == 0 else west[side] - east[side]
                 for side in range(2)
             ]
             for parity in range(2):
                 value = north + south if parity == 0 else north - south
+                if kind == 0:
+                    left, right = value[:, :quarter], value[:, quarter:]
+                    value = jnp.concatenate([left + right, left - right], axis=1)
                 place = (field * 2 + parity + turn) & 3
                 at = pl.multiple_of(place * rows + row, 16)
-                folded[pl.ds(at, 16), :] = value.astype(jnp.bfloat16)
-
+                folded[kind, pl.ds(at, 16), :] = value.astype(jnp.bfloat16)
+
+    def product(first, second):
+        return lax.dot_general(first, second, NT, preferred_element_type=jnp.float32).astype(
+            jnp.bfloat16
+        )
+
+    for field in range(fields):
+        grid_copies[field].wait()
+        fold(0, field)
+    table_copies[0].wait()
+    waves = table.shape[1]
+    half_rows = waves // 2
+    for which in range(2):
+        lanes = slice(which * quarter, (which + 1) * quarter)
+        got = product(table_here[0, :, lanes], folded[0, :, lanes])
+        for part in range(2):
+            out[part, which * half_rows : (which + 1) * half_rows] = got[
+                part * half_rows : (part + 1) * half_rows
+            ]
+    for field in range(fields):
+        fold(1, field)
     for part in range(2):
-        out[part] = lax.dot_general(
-            table[part], folded[...], NT, preferred_element_type=jnp.float32
-        ).astype(jnp.bfloat16)
+        table_copies[1 + part].wait()
+    got = product(table_here[1:].reshape(2 * waves, half), folded[1])
+    for part in range(2):
+        out[2 + part] = got[part * waves : (part + 1) * waves]
 
 
 def transform(me, grid_fields, table):
     fields, _, rows, lons = grid_fields.shape
-    kinds, waves, half = table.shape
+    parts, waves, half = table.shape
     lanes = fields * 2 * rows
     return pl.pallas_call(
         transform_kernel,
-        grid_spec=pltpu.PrefetchScalarGridSpec(
-            num_scalar_prefetch=1,
-            grid=(2,),
-            in_specs=[
-                pl.BlockSpec(grid_fields.shape, lambda k, me: (0, 0, 0, 0)),
-                pl.BlockSpec((2, waves, half), lambda k, me: (k, 0, 0)),
-            ],
-            out_specs=pl.BlockSpec((2, waves, lanes), lambda k, me: (k, 0, 0)),
-            scratch_shapes=[pltpu.VMEM((lanes, half), jnp.bfloat16)],
-        ),
-        out_shape=jax.ShapeDtypeStruct((kinds, waves, lanes), jnp.bfloat16),
+        in_specs=[
+            pl.BlockSpec(memory_space=pltpu.SMEM),
+            pl.BlockSpec(memory_space=pl.ANY),
+            pl.BlockSpec(memory_space=pl.ANY),
+        ],
+        out_specs=pl.BlockSpec(memory_space=pltpu.VMEM),
+        scratch_shapes=[
+            pltpu.VMEM(grid_fields.shape, jnp.bfloat16),
+            pltpu.VMEM(table.shape, jnp.bfloat16),
+            pltpu.VMEM((2, lanes, half), jnp.bfloat16),
+            pltpu.SemaphoreType.DMA((fields,)),
+            pltpu.SemaphoreType.DMA((parts,)),
+        ],
+        out_shape=jax.ShapeDtypeStruct((4, waves, lanes), jnp.bfloat16),
         compiler_params=pltpu.CompilerParams(vmem_limit_bytes=24 << 20),
         cost_estimate=pl.CostEstimate(
-            flops=2 * kinds * waves * half * lanes, bytes_accessed=10 << 20, transcendentals=0
+            flops=6 * waves * half * lanes, bytes_accessed=10 << 20, transcendentals=0
         ),
         name="transform",
     )(me, grid_fields, table)
 
 
-def order_kernel(waves, fourier, out, square, picks, rows_f32):
+def transform_table(lon_count):
+    full = half_table(lon_count, quarter_order(np.arange(MM // 2)))
+    short = full[0, :, :, : lon_count // 4].reshape(2, 2, MM // 4, lon_count // 4)
+    short = short.transpose(0, 2, 1, 3).reshape(MM // 2, lon_count // 2)
+    return np.stack([short, full[1, 0], full[1, 1]])
+
+
+def order_kernel(waves, fourier, out, square, picks, rows_f32, staged, sems):
     kinds, count, lanes = fourier.shape
     devices, size, _ = out.shape
     pairs = size // kinds
@@ -152,7 +200,7 @@
     for device in range(devices):
         square[device : device + 1, : 2 * pairs] = waves[device]
     square[...] = square[...].T
-    number = lax.broadcasted_iota(jnp.int32, (pairs, count), 1)
+    number = quarter_order(lax.broadcasted_iota(jnp.int32, (pairs, count), 1))
     firsts = square[pl.ds(0, pairs, stride=2), :]
     for device in range(devices):
         wave = firsts[:, device : device + 1]
@@ -163,11 +211,19 @@
         got = jnp.dot(picks[...], fourier[kind], preferred_element_type=jnp.float32)
         for tile in range(lanes // 128):
             rows_f32[tile, pl.ds(kind, slots, stride=kinds), :] = got[:, tile * 128 : tile * 128 + 128]
+    copies = []
     for device in range(devices):
         for tile in range(lanes // 128):
-            out[device, :, tile * 128 : tile * 128 + 128] = rows_f32[
+            staged[device, :, tile * 128 : tile * 128 + 128] = rows_f32[
                 tile, device * size : (device + 1) * size, :
             ].astype(jnp.bfloat16)
+        if device % 8 == 7:
+            part = pl.ds(device - 7, 8)
+            copy = pltpu.make_async_copy(staged.at[part], out.at[part], sems.at[device // 8])
+            copy.start()
+            copies.append(copy)
+    for copy in copies:
+        copy.wait()
 
 
 def ordered(waves, fourier, pairs):
@@ -178,11 +234,13 @@
     return pl.pallas_call(
         order_kernel,
         in_specs=[whole, whole],
-        out_specs=whole,
+        out_specs=pl.BlockSpec(memory_space=pl.ANY),
         scratch_shapes=[
             pltpu.VMEM((128, 128), jnp.int32),
             pltpu.VMEM((slots, count), jnp.bfloat16),
             pltpu.VMEM((lanes // 128, kinds * slots, 128), jnp.float32),
+            pltpu.VMEM((devices, kinds * pairs, lanes), jnp.bfloat16),
+            pltpu.SemaphoreType.DMA((devices // 8,)),
         ],
         out_shape=jax.ShapeDtypeStruct((devices, kinds * pairs, lanes), jnp.bfloat16),
         compiler_params=pltpu.CompilerParams(vmem_limit_bytes=24 << 20),
@@ -223,7 +281,7 @@
     )(table)
 
 
-def legendre_kernel(waves, blocks, table, last, spread, out, held, data, lines, sems):
+def legendre_kernel(waves, blocks, table, last, spread, out, held, data, lines, staged, sems, out_sems):
     pairs, lat, wide = table.shape
     lanes = blocks.shape[2]
     rows = lanes // 4
@@ -259,12 +317,29 @@
                                 half * lanes : (half + 1) * lanes,
                             ] = value[pair * 4 + kind * 2 : pair * 4 + kind * 2 + 2]
 
+    for pair in range(pairs):
+        wave = waves[pair]
+        for side in range(2):
+            value = jnp.sum(
+                data[pair, side] * last[pair, side : side + 1].astype(jnp.float32), axis=1, keepdims=True
+            )
+            first_count = (MM - wave + 1 - side) >> 1
+            second_count = (wave + 2 - side) >> 1
+            live = (columns - 1 < first_count + second_count) & (wave < MM)
+            in_first = jnp.where(columns - 1 < first_count, 1, 0)
+            value = jnp.where(in_first != (wave & 1), value[:16], value[16:])
+            value = jnp.where(live, value, 0.0).astype(jnp.bfloat16)
+            staged[pair, side, :, :, columns - 1 :] = value.reshape(8, 2, 1)
+
     index = lax.broadcasted_iota(jnp.int32, (32, wide), 1)
     even = index & 1 == 0
     index = index[:16]
     parity, column = index & 1, index >> 1
-    for group in range(pairs // GROUP):
-        for pair in range(group * GROUP, (group + 1) * GROUP):
+    written = []
+    groups = [GROUP] * (pairs // GROUP - 1) + [GROUP // 2, GROUP // 4, GROUP // 4]
+    for group, count in enumerate(groups):
+        start = sum(groups[:group])
+        for pair in range(start, start + count):
             copies[pair].wait()
             if pair + AHEAD < pairs:
                 copies[pair + AHEAD].start()
@@ -279,32 +354,24 @@
             value = jnp.where(in_first != (wave & 1), value[:16], value[16:])
             lines[pair * 16 : pair * 16 + 16, :] = jnp.where(live, value, 0.0).astype(jnp.bfloat16)
 
-        top = group * GROUP * 16
+        top = start * 16
         for block in range(wide // 256):
             apart = jnp.dot(
-                lines[top : top + GROUP * 16, block * 256 : block * 256 + 256],
+                lines[top : top + count * 16, block * 256 : block * 256 + 256],
                 spread[...],
                 preferred_element_type=jnp.float32,
             ).astype(jnp.bfloat16)
-            for pair in range(GROUP):
+            for pair in range(count):
                 for side in range(2):
                     piece = apart[pair * 16 : pair * 16 + 16, side * 128 : side * 128 + 128]
-                    out[group * GROUP + pair, side, :, :, block * 128 : block * 128 + 128] = (
+                    staged[start + pair, side, :, :, block * 128 : block * 128 + 128] = (
                         piece.reshape(8, 2, 128)
                     )
-    for pair in range(pairs):
-        wave = waves[pair]
-        for side in range(2):
-            value = jnp.sum(
-                data[pair, side] * last[pair, side : side + 1].astype(jnp.float32), axis=1, keepdims=True
-            )
-            first_count = (MM - wave + 1 - side) >> 1
-            second_count = (wave + 2 - side) >> 1
-            live = (columns - 1 < first_count + second_count) & (wave < MM)
-            in_first = jnp.where(columns - 1 < first_count, 1, 0)
-            value = jnp.where(in_first != (wave & 1), value[:16], value[16:])
-            value = jnp.where(live, value, 0.0).astype(jnp.bfloat16)
-            out[pair, side, :, :, columns - 1 :] = value.reshape(8, 2, 1)
+        part = pl.ds(start, count)
+        written.append(pltpu.make_async_copy(staged.at[part], out.at[part], out_sems.at[group]))
+        written[-1].start()
+    for copy in written:
+        copy.wait()
 
 
 def legendre_product(waves, blocks, table, last):
@@ -323,12 +390,14 @@
             whole,
             whole,
         ],
-        out_specs=whole,
+        out_specs=pl.BlockSpec(memory_space=pl.ANY),
         scratch_shapes=[
             pltpu.VMEM((pairs, lat, wide), jnp.bfloat16),
             pltpu.VMEM((pairs, 2, 32, lat), jnp.float32),
             pltpu.VMEM((16 * pairs, wide), jnp.bfloat16),
+            pltpu.VMEM((pairs, 2, 8, 2, columns), jnp.bfloat16),
             pltpu.SemaphoreType.DMA((pairs,)),
+            pltpu.SemaphoreType.DMA((pairs // GROUP + 2,)),
         ],
         out_shape=jax.ShapeDtypeStruct((pairs, 2, 8, 2, columns), jnp.bfloat16),
         compiler_params=pltpu.CompilerParams(vmem_limit_bytes=48 << 20),
@@ -343,7 +412,7 @@
     me = lax.axis_index(AXES).astype(jnp.int32).reshape(1)
     own_waves = slot_wave.reshape(own_pairs, 2)[:, 0]
     waves = lax.all_to_all(repeated(slot_wave, devices), AXES, 0, 0, tiled=True)
-    table = jnp.asarray(half_table(lon_count).reshape(4, MM // 2, lon_count // 2))
+    table = jnp.asarray(transform_table(lon_count))
     fourier = transform(me, HBM(grid_fields), HBM(table))
     sent = ordered(waves, fourier, own_pairs)
     got = lax.all_to_all(sent, AXES, 0, 0, tiled=True)

time: 73.2 us -> 72.5 us (level)
  Pallas kernels: 38.9 us -> 38.1 us
    pallas_call x2, Pallas kernels: 9.34 us -> 8.47 us  [the longest x1 5.84 us: transform(): pl.pallas_call(transform_kernel, in_specs=[pl.BlockSpec(memory_space=pltp...]
  transfers between devices with their start and end apart: 2 -> 2, of which waited for: 2 -> 2; matrix products, arithmetic and copies ran while one was open for 0% -> 0% of each run, Pallas kernels for 32% -> 31%
where the time goes in v3:
time: 72.5 us; the launch traced here: 72.1 us
  Pallas kernels  38.1 us (53%)
  waiting for transfers between devices  13.5 us (19%)
  starting transfers between devices  11.9 us (16%)
  local copies, waits for them, and re-layouts  8.5 us (12%)
    pallas_call x1, Pallas kernels, turned(): pl.pallas_call(turned_kernel, grid=(pairs,), in_specs=[pl.BlockSpec((1, c...  16.7 us
    all_to_all x1, waiting for transfers between devices, local(): got = lax.all_to_all(sent, AXES, 0, 0, tiled=True)  12.2 us
    pallas_call x1, Pallas kernels, legendre_product(): pl.pallas_call(legendre_kernel, in_specs=[pl.BlockSpec(memory_space=pltpu...  11.6 us
    unnamed x6, local copies, waits for them, and re-layouts  8.31 us
    all_to_all x1, starting transfers between devices, local(): waves = lax.all_to_all(repeated(slot_wave, devices), AXES, 0, 0, tiled=True)  7.3 us
    pallas_call x1, Pallas kernels, transform(): pl.pallas_call(transform_kernel, in_specs=[pl.BlockSpec(memory_space=pltp...  5.84 us
    all_to_all x1, starting transfers between devices, local(): got = lax.all_to_all(sent, AXES, 0, 0, tiled=True)  4.63 us
    pallas_call x1, Pallas kernels, ordered(): pl.pallas_call(order_kernel, in_specs=[whole, whole], out_specs=pl.BlockS...  2.63 us
  transfers between devices with their start and end apart: 2, of which 2 were waited for; matrix products, arithmetic and copies ran while one was open for 0% of the time, Pallas kernels for 31%

profile of v3, /device:TPU:0, one launch (start us, length us, event | category | flops | bytes accessed | tf_op | source)
XLA Modules:
  0.0 72.1 jit_solution(18019715761548696743)
XLA Ops:
  0.0 1.3 %repeated.1 = s32[32,1,32]{2,1,0:T(1,128)} custom-call(s32[1,1,32]{2,1,0:T(1,128)} %bitcast.3), custom_call_target="tpu_custom_call" | custom-call | tf_op jit(solution)/shard_map/repeated/pallas_call | solution.py:84
  1.3 7.3 %all-to-all-start = ((s32[32,1,32]{2,1,0:T(1,128)}), s32[32,1,32]{2,1,0:T(1,128)S(1)}, u32[]{:S(2)}, u32[]{:S(2)}) async-start(s32[32,1,32]{2,1,0:T(1,128)} %repeated.1), calls=%async_computation | async-start | bytes 32768 | tf_op jit(solution)/shard_map/all_to_all | solution.py:414
  8.6 5.8 %transform.1.fourier = bf16[4,512,384]{2,1,0:T(8,128)(2,1)S(1)} custom-call(s32[1]{0:T(128)} %bitcast.1.me, bf16[2,2,96,3072]{3,2,1,0:T(8,128)(2,1)} %grid.1, bf16[3,512,1536]{2,1,0:T(8,128)(2,1)} %constant.15.clone.table), custom_call_target="tpu_custom_call" | custom-call | flops 1811939328 | bytes 10485760 | tf_op jit(solution)/shard_map/transform/pallas_call | solution.py:163
  14.4 1.2 %all-to-all-done.waves = s32[32,1,32]{2,1,0:T(1,128)S(1)} async-done(((s32[32,1,32]{2,1,0:T(1,128)}), s32[32,1,32]{2,1,0:T(1,128)S(1)}, u32[]{:S(2)}, u32[]{:S(2)}) %all-to-all-start) | async-done | bytes 4128 | tf_op jit(solution)/shard_map/all_to_all | solution.py:414
  15.6 2.6 %ordered.1 = bf16[32,64,384]{2,1,0:T(8,128)(2,1)} custom-call(s32[32,1,32]{2,1,0:T(1,128)S(1)} %all-to-all-done.waves, bf16[4,512,384]{2,1,0:T(8,128)(2,1)S(1)} %transform.1.fourier), custom_call_target="tpu_custom_call" | custom-call | flops 805306368 | bytes 4194304 | tf_op jit(solution)/shard_map/ordered/pallas_call | solution.py:234
  18.3 0.0 copy-start.2
  18.3 4.6 %all-to-all-start.1 = ((bf16[32,64,384]{2,1,0:T(8,128)(2,1)}), bf16[32,64,384]{2,1,0:T(8,128)(2,1)S(1)}, u32[]{:S(2)}, u32[]{:S(2)}) async-start(bf16[32,64,384]{2,1,0:T(8,128)(2,1)} %ordered.1), calls=%async_computation.1 | async-start | bytes 3145728 | tf_op jit(solution)/shard_map/all_to_all | solution.py:418
  22.9 0.0 copy-done.2
  22.9 0.1 reshape.9
  23.0 0.1 slice_reduce_fusion.waves
  23.2 0.0 copy-start
  23.2 16.7 %turned.1 = (bf16[16,768,1024]{2,1,0:T(8,128)(2,1)S(1)}, bf16[16,2,768]{2,1,0:T(2,128)(2,1)S(1)}) custom-call(bf16[16,513,2,768]{3,2,1,0:T(2,128)(2,1)} %bitcast.4), custom_call_target="tpu_custom_call" | custom-call | flops 21474836480 | bytes 62914560 | tf_op jit(solution)/shard_map/turned/pallas_call | solution.py:264
  39.9 0.0 copy-start.1
  39.9 8.3 %copy-done.1 = bf16[16,768,1024]{2,1,0:T(8,128)(2,1)} copy-done((bf16[16,768,1024]{2,1,0:T(8,128)(2,1)}, bf16[16,768,1024]{2,1,0:T(8,128)(2,1)S(1)}, u32[]{:S(2)}) %copy-start.1) | copy-done | bytes 25165848
  48.2 12.2 %all-to-all-done.1.blocks = bf16[32,64,384]{2,1,0:T(8,128)(2,1)S(1)} async-done(((bf16[32,64,384]{2,1,0:T(8,128)(2,1)}), bf16[32,64,384]{2,1,0:T(8,128)(2,1)S(1)}, u32[]{:S(2)}, u32[]{:S(2)}) %all-to-all-start.1) | async-done | bytes 1572896 | tf_op jit(solution)/shard_map/all_to_all | solution.py:418
  60.5 0.0 copy-done
  60.5 11.6 %legendre_product.1 = bf16[16,2,8,2,513]{4,3,2,1,0:T(2,128)(2,1)} custom-call(s32[16]{0:T(128)S(1)} %slice_reduce_fusion.waves, bf16[32,64,384]{2,1,0:T(8,128)(2,1)S(1)} %all-to-all-done.1.blocks, bf16[16,768,1024]{2,1,0:T(8,128)(2,1)} %copy-done.1, bf16[16,2,768]{2,1,0:T(2,128)(2,1)S(1)} %get-tuple-element.8.last, bf16[256,256]{1,0:T(8,128)(2,1)S(1)} %copy-done), custom_call_target="tpu_custom_call" | custom-call | flops 8589934592 | bytes 31457280 | tf_op jit(solution)/shard_map/legendre_product/pallas_call | solution.py:384
Async XLA Ops:
  1.3 14.4 %all-to-all-start = ((s32[32,1,32]{2,1,0:T(1,128)}), s32[32,1,32]{2,1,0:T(1,128)S(1)}, u32[]{:S(2)}, u32[]{:S(2)}) async-start(s32[32,1,32]{2,1,0:T(1,128)} %repeated.1), calls=%async_computation | async-start | bytes 32768 | tf_op jit(solution)/shard_map/all_to_all | solution.py:414
  18.3 4.7 %copy-start.2 = (s32[32]{0:T(128)S(1)}, s32[32]{0:T(128)}, u32[]{:S(2)}) copy-start(s32[32]{0:T(128)} %param.7) | copy-start | bytes 388
  18.3 42.2 %all-to-all-start.1 = ((bf16[32,64,384]{2,1,0:T(8,128)(2,1)}), bf16[32,64,384]{2,1,0:T(8,128)(2,1)S(1)}, u32[]{:S(2)}, u32[]{:S(2)}) async-start(bf16[32,64,384]{2,1,0:T(8,128)(2,1)} %ordered.1), calls=%async_computation.1 | async-start | bytes 3145728 | tf_op jit(solution)/shard_map/all_to_all | solution.py:418
  23.2 37.3 %copy-start = (bf16[256,256]{1,0:T(8,128)(2,1)S(1)}, bf16[256,256]{1,0:T(8,128)(2,1)}, u32[]{:S(2)}) copy-start(bf16[256,256]{1,0:T(8,128)(2,1)} %constant.16.clone.spread) | copy-start | bytes 393220
  39.9 8.3 %copy-start.1 = (bf16[16,768,1024]{2,1,0:T(8,128)(2,1)}, bf16[16,768,1024]{2,1,0:T(8,128)(2,1)S(1)}, u32[]{:S(2)}) copy-start(bf16[16,768,1024]{2,1,0:T(8,128)(2,1)S(1)} %get-tuple-element.7.table) | copy-start | bytes 75497472

commit v4 on v3

--- a/solution.py
+++ b/solution.py
@@ -72,7 +72,7 @@
 
 NT = (((1,), (1,)), ((), ()))
 GROUP = 4
-AHEAD = 16
+HEAD = 1
 
 
 def repeat_kernel(wave, out):
@@ -251,10 +251,20 @@
     )(waves, fourier)
 
 
-def turned_kernel(table, out, last):
+def turned_kernel(table, head, out, last):
     columns, _, lat = table.shape[1:]
     main = columns - 1
-    out[0] = table[0, :main].reshape(2 * main, lat).T
+    step = pl.program_id(0)
+    value = table[0, :main].reshape(2 * main, lat).T
+
+    @pl.when(step < HEAD)
+    def _():
+        head[jnp.minimum(step, HEAD - 1)] = value
+
+    @pl.when(step >= HEAD)
+    def _():
+        out[0] = value
+
     last[0] = table[0, main]
 
 
@@ -266,14 +276,16 @@
         grid=(pairs,),
         in_specs=[pl.BlockSpec((1, columns, 2, lat), lambda i: (i, 0, 0, 0))],
         out_specs=[
-            pl.BlockSpec((1, lat, wide), lambda i: (i, 0, 0)),
+            pl.BlockSpec((HEAD, lat, wide), lambda i: (0, 0, 0)),
+            pl.BlockSpec((1, lat, wide), lambda i: (jnp.maximum(i - HEAD, 0), 0, 0)),
             pl.BlockSpec((1, 2, lat), lambda i: (i, 0, 0)),
         ],
         out_shape=[
-            jax.ShapeDtypeStruct((pairs, lat, wide), jnp.bfloat16),
+            jax.ShapeDtypeStruct((HEAD, lat, wide), jnp.bfloat16),
+            jax.ShapeDtypeStruct((pairs - HEAD, lat, wide), jnp.bfloat16),
             jax.ShapeDtypeStruct((pairs, 2, lat), jnp.bfloat16),
         ],
-        compiler_params=pltpu.CompilerParams(vmem_limit_bytes=16 << 20),
+        compiler_params=pltpu.CompilerParams(vmem_limit_bytes=24 << 20),
         cost_estimate=pl.CostEstimate(
             flops=20 << 30, bytes_accessed=60 << 20, transcendentals=0
         ),
@@ -281,16 +293,18 @@
     )(table)
 
 
-def legendre_kernel(waves, blocks, table, last, spread, out, held, data, lines, staged, sems, out_sems):
-    pairs, lat, wide = table.shape
+def legendre_kernel(waves, blocks, head, table, last, spread, out, held, data, lines, staged, sems, out_sems):
+    lat, wide = table.shape[1:]
+    pairs = last.shape[0]
     lanes = blocks.shape[2]
     rows = lanes // 4
     columns = wide // 2 + 1
     copies = [
-        pltpu.make_async_copy(table.at[pair], held.at[pair], sems.at[pair]) for pair in range(pairs)
+        pltpu.make_async_copy(table.at[pair], held.at[pair], sems.at[pair])
+        for pair in range(pairs - HEAD)
     ]
-    for pair in range(AHEAD):
-        copies[pair].start()
+    for copy in copies:
+        copy.start()
     lane = lax.broadcasted_iota(jnp.int32, (4 * GROUP, lanes), 1)
     for group in range(pairs // GROUP):
         for half in range(2):
@@ -340,11 +354,11 @@
     for group, count in enumerate(groups):
         start = sum(groups[:group])
         for pair in range(start, start + count):
-            copies[pair].wait()
-            if pair + AHEAD < pairs:
-                copies[pair + AHEAD].start()
+            if pair >= HEAD:
+                copies[pair - HEAD].wait()
+            matrix = head[pair] if pair < HEAD else held[pair - HEAD]
             here = data[pair].reshape(64, lat).astype(jnp.bfloat16)
-            both = jnp.dot(here, held[pair], preferred_element_type=jnp.float32)
+            both = jnp.dot(here, matrix, preferred_element_type=jnp.float32)
             value = jnp.where(even, both[:32], both[32:])
             wave = waves[pair]
             first_count = (MM - wave + 1 - parity) >> 1
@@ -374,8 +388,9 @@
         copy.wait()
 
 
-def legendre_product(waves, blocks, table, last):
-    pairs, lat, wide = table.shape
+def legendre_product(waves, blocks, head, table, last):
+    lat, wide = table.shape[1:]
+    pairs = last.shape[0]
     columns = wide // 2 + 1
     lane = np.arange(256)
     spread = np.zeros((256, 256), np.float32)
@@ -386,24 +401,25 @@
         in_specs=[
             pl.BlockSpec(memory_space=pltpu.SMEM),
             whole,
+            whole,
             pl.BlockSpec(memory_space=pl.ANY),
             whole,
             whole,
         ],
         out_specs=pl.BlockSpec(memory_space=pl.ANY),
         scratch_shapes=[
-            pltpu.VMEM((pairs, lat, wide), jnp.bfloat16),
+            pltpu.VMEM(table.shape, jnp.bfloat16),
             pltpu.VMEM((pairs, 2, 32, lat), jnp.float32),
             pltpu.VMEM((16 * pairs, wide), jnp.bfloat16),
             pltpu.VMEM((pairs, 2, 8, 2, columns), jnp.bfloat16),
-            pltpu.SemaphoreType.DMA((pairs,)),
+            pltpu.SemaphoreType.DMA((pairs - HEAD,)),
             pltpu.SemaphoreType.DMA((pairs // GROUP + 2,)),
         ],
         out_shape=jax.ShapeDtypeStruct((pairs, 2, 8, 2, columns), jnp.bfloat16),
         compiler_params=pltpu.CompilerParams(vmem_limit_bytes=48 << 20),
         cost_estimate=pl.CostEstimate(flops=8 << 30, bytes_accessed=30 << 20, transcendentals=0),
         name="legendre_product",
-    )(waves, blocks, table, last, jnp.asarray(spread.astype(jnp.bfloat16)))
+    )(waves, blocks, head, table, last, jnp.asarray(spread.astype(jnp.bfloat16)))
 
 
 def local(grid_fields, legendre, slot_wave, *, devices):
@@ -416,8 +432,8 @@
     fourier = transform(me, HBM(grid_fields), HBM(table))
     sent = ordered(waves, fourier, own_pairs)
     got = lax.all_to_all(sent, AXES, 0, 0, tiled=True)
-    rows, last = turned(HBM(legendre.transpose(0, 3, 1, 2)))
-    return legendre_product(own_waves, got, HBM(rows), last)
+    head, rows, last = turned(HBM(legendre.transpose(0, 3, 1, 2)))
+    return legendre_product(own_waves, got, head, HBM(rows), last)
 
 
 def HBM(array):

time: 72.5 us -> 72 us (level)
  transfers between devices with their start and end apart: 2 -> 2, of which waited for: 2 -> 2; matrix products, arithmetic and copies ran while one was open for 0% -> 0% of each run, Pallas kernels for 31% -> 32%
where the time goes in v4:
time: 72 us; the launch traced here: 71.7 us
  Pallas kernels  38.3 us (53%)
  waiting for transfers between devices  13.4 us (19%)
  starting transfers between devices  11.9 us (17%)
  local copies, waits for them, and re-layouts  8 us (11%)
    pallas_call x1, Pallas kernels, turned(): pl.pallas_call(turned_kernel, grid=(pairs,), in_specs=[pl.BlockSpec((1, c...  17.4 us
    all_to_all x1, waiting for transfers between devices, local(): got = lax.all_to_all(sent, AXES, 0, 0, tiled=True)  12.1 us
    pallas_call x1, Pallas kernels, legendre_product(): pl.pallas_call(legendre_kernel, in_specs=[pl.BlockSpec(memory_space=pltpu...  11.2 us
    unnamed x6, local copies, waits for them, and re-layouts  7.8 us
    all_to_all x1, starting transfers between devices, local(): waves = lax.all_to_all(repeated(slot_wave, devices), AXES, 0, 0, tiled=True)  7.3 us
    pallas_call x1, Pallas kernels, transform(): pl.pallas_call(transform_kernel, in_specs=[pl.BlockSpec(memory_space=pltp...  5.84 us
    all_to_all x1, starting transfers between devices, local(): got = lax.all_to_all(sent, AXES, 0, 0, tiled=True)  4.63 us
    pallas_call x1, Pallas kernels, ordered(): pl.pallas_call(order_kernel, in_specs=[whole, whole], out_specs=pl.BlockS...  2.57 us
  transfers between devices with their start and end apart: 2, of which 2 were waited for; matrix products, arithmetic and copies ran while one was open for 0% of the time, Pallas kernels for 32%

profile of v4, /device:TPU:0, one launch (start us, length us, event | category | flops | bytes accessed | tf_op | source)
XLA Modules:
  0.0 71.7 jit_solution(13041453968738684359)
XLA Ops:
  0.0 1.3 %repeated.1 = s32[32,1,32]{2,1,0:T(1,128)} custom-call(s32[1,1,32]{2,1,0:T(1,128)} %bitcast.3), custom_call_target="tpu_custom_call" | custom-call | tf_op jit(solution)/shard_map/repeated/pallas_call | solution.py:84
  1.3 7.3 %all-to-all-start = ((s32[32,1,32]{2,1,0:T(1,128)}), s32[32,1,32]{2,1,0:T(1,128)S(1)}, u32[]{:S(2)}, u32[]{:S(2)}) async-start(s32[32,1,32]{2,1,0:T(1,128)} %repeated.1), calls=%async_computation | async-start | bytes 32768 | tf_op jit(solution)/shard_map/all_to_all | solution.py:430
  8.6 5.8 %transform.1.fourier = bf16[4,512,384]{2,1,0:T(8,128)(2,1)S(1)} custom-call(s32[1]{0:T(128)} %bitcast.1.me, bf16[2,2,96,3072]{3,2,1,0:T(8,128)(2,1)} %grid.1, bf16[3,512,1536]{2,1,0:T(8,128)(2,1)} %constant.15.clone.table), custom_call_target="tpu_custom_call" | custom-call | flops 1811939328 | bytes 10485760 | tf_op jit(solution)/shard_map/transform/pallas_call | solution.py:163
  14.4 1.2 %all-to-all-done.waves = s32[32,1,32]{2,1,0:T(1,128)S(1)} async-done(((s32[32,1,32]{2,1,0:T(1,128)}), s32[32,1,32]{2,1,0:T(1,128)S(1)}, u32[]{:S(2)}, u32[]{:S(2)}) %all-to-all-start) | async-done | bytes 4128 | tf_op jit(solution)/shard_map/all_to_all | solution.py:430
  15.6 2.6 %ordered.1 = bf16[32,64,384]{2,1,0:T(8,128)(2,1)} custom-call(s32[32,1,32]{2,1,0:T(1,128)S(1)} %all-to-all-done.waves, bf16[4,512,384]{2,1,0:T(8,128)(2,1)S(1)} %transform.1.fourier), custom_call_target="tpu_custom_call" | custom-call | flops 805306368 | bytes 4194304 | tf_op jit(solution)/shard_map/ordered/pallas_call | solution.py:234
  18.2 0.0 copy-start.2
  18.2 4.6 %all-to-all-start.1 = ((bf16[32,64,384]{2,1,0:T(8,128)(2,1)}), bf16[32,64,384]{2,1,0:T(8,128)(2,1)S(1)}, u32[]{:S(2)}, u32[]{:S(2)}) async-start(bf16[32,64,384]{2,1,0:T(8,128)(2,1)} %ordered.1), calls=%async_computation.1 | async-start | bytes 3145728 | tf_op jit(solution)/shard_map/all_to_all | solution.py:434
  22.9 0.0 copy-done.2
  22.9 0.1 reshape.9
  23.0 0.1 slice_reduce_fusion.waves
  23.1 0.0 copy-start
  23.1 17.4 %turned.1 = (bf16[1,768,1024]{2,1,0:T(8,128)(2,1)S(1)}, bf16[15,768,1024]{2,1,0:T(8,128)(2,1)S(1)}, bf16[16,2,768]{2,1,0:T(2,128)(2,1)S(1)}) custom-call(bf16[16,513,2,768]{3,2,1,0:T(2,128)(2,1)} %bitcast.4), custom_call_target="tpu_custom_call" | custom-call | flops 21474836480 | bytes 62914560 | tf_op jit(solution)/shard_map/turned/pallas_call | solution.py:274
  40.5 0.0 copy-start.1
  40.5 7.8 %copy-done.1 = bf16[15,768,1024]{2,1,0:T(8,128)(2,1)} copy-done((bf16[15,768,1024]{2,1,0:T(8,128)(2,1)}, bf16[15,768,1024]{2,1,0:T(8,128)(2,1)S(1)}, u32[]{:S(2)}) %copy-start.1) | copy-done | bytes 23592984
  48.3 12.1 %all-to-all-done.1.blocks = bf16[32,64,384]{2,1,0:T(8,128)(2,1)S(1)} async-done(((bf16[32,64,384]{2,1,0:T(8,128)(2,1)}), bf16[32,64,384]{2,1,0:T(8,128)(2,1)S(1)}, u32[]{:S(2)}, u32[]{:S(2)}) %all-to-all-start.1) | async-done | bytes 1572896 | tf_op jit(solution)/shard_map/all_to_all | solution.py:434
  60.4 0.0 copy-done
  60.4 11.2 %legendre_product.1 = bf16[16,2,8,2,513]{4,3,2,1,0:T(2,128)(2,1)} custom-call(s32[16]{0:T(128)S(1)} %slice_reduce_fusion.waves, bf16[32,64,384]{2,1,0:T(8,128)(2,1)S(1)} %all-to-all-done.1.blocks, bf16[1,768,1024]{2,1,0:T(8,128)(2,1)S(1)} %get-tuple-element.8.head, bf16[15,768,1024]{2,1,0:T(8,128)(2,1)} %copy-done.1, ...), custom_call_target="tpu_custom_call" | custom-call | flops 8589934592 | bytes 31457280 | tf_op jit(solution)/shard_map/legendre_product/pallas_call | solution.py:399
Async XLA Ops:
  1.3 14.4 %all-to-all-start = ((s32[32,1,32]{2,1,0:T(1,128)}), s32[32,1,32]{2,1,0:T(1,128)S(1)}, u32[]{:S(2)}, u32[]{:S(2)}) async-start(s32[32,1,32]{2,1,0:T(1,128)} %repeated.1), calls=%async_computation | async-start | bytes 32768 | tf_op jit(solution)/shard_map/all_to_all | solution.py:430
  18.2 4.7 %copy-start.2 = (s32[32]{0:T(128)S(1)}, s32[32]{0:T(128)}, u32[]{:S(2)}) copy-start(s32[32]{0:T(128)} %param.7) | copy-start | bytes 388
  18.2 42.2 %all-to-all-start.1 = ((bf16[32,64,384]{2,1,0:T(8,128)(2,1)}), bf16[32,64,384]{2,1,0:T(8,128)(2,1)S(1)}, u32[]{:S(2)}, u32[]{:S(2)}) async-start(bf16[32,64,384]{2,1,0:T(8,128)(2,1)} %ordered.1), calls=%async_computation.1 | async-start | bytes 3145728 | tf_op jit(solution)/shard_map/all_to_all | solution.py:434
  23.1 37.3 %copy-start = (bf16[256,256]{1,0:T(8,128)(2,1)S(1)}, bf16[256,256]{1,0:T(8,128)(2,1)}, u32[]{:S(2)}) copy-start(bf16[256,256]{1,0:T(8,128)(2,1)} %constant.16.clone.spread) | copy-start | bytes 393220
  40.5 7.8 %copy-start.1 = (bf16[15,768,1024]{2,1,0:T(8,128)(2,1)}, bf16[15,768,1024]{2,1,0:T(8,128)(2,1)S(1)}, u32[]{:S(2)}) copy-start(bf16[15,768,1024]{2,1,0:T(8,128)(2,1)S(1)} %get-tuple-element.9.table) | copy-start | bytes 70778880

commit v5 on v4

--- a/solution.py
+++ b/solution.py
@@ -207,21 +207,29 @@
         picks[device * pairs : (device + 1) * pairs, :] = (
             jnp.where(wave == number, 1.0, 0.0).astype(jnp.bfloat16)
         )
-    for kind in range(kinds):
-        got = jnp.dot(picks[...], fourier[kind], preferred_element_type=jnp.float32)
-        for tile in range(lanes // 128):
-            rows_f32[tile, pl.ds(kind, slots, stride=kinds), :] = got[:, tile * 128 : tile * 128 + 128]
     copies = []
-    for device in range(devices):
-        for tile in range(lanes // 128):
-            staged[device, :, tile * 128 : tile * 128 + 128] = rows_f32[
-                tile, device * size : (device + 1) * size, :
-            ].astype(jnp.bfloat16)
-        if device % 8 == 7:
-            part = pl.ds(device - 7, 8)
-            copy = pltpu.make_async_copy(staged.at[part], out.at[part], sems.at[device // 8])
-            copy.start()
-            copies.append(copy)
+    share = 8
+    for first in range(0, devices, share):
+        for kind in range(kinds):
+            got = jnp.dot(
+                picks[first * pairs : (first + share) * pairs, :],
+                fourier[kind],
+                preferred_element_type=jnp.float32,
+            )
+            for tile in range(lanes // 128):
+                rows_f32[tile, pl.ds(first * size + kind, share * pairs, stride=kinds), :] = got[
+                    :, tile * 128 : tile * 128 + 128
+                ]
+        for device in range(first, first + share):
+            for tile in range(lanes // 128):
+                staged[device, :, tile * 128 : tile * 128 + 128] = rows_f32[
+                    tile, device * size : (device + 1) * size, :
+                ].astype(jnp.bfloat16)
+        part = pl.ds(first, share)
+        copies.append(
+            pltpu.make_async_copy(staged.at[part], out.at[part], sems.at[first // share])
+        )
+        copies[-1].start()
     for copy in copies:
         copy.wait()
 
@@ -293,7 +301,10 @@
     )(table)
 
 
-def legendre_kernel(waves, blocks, head, table, last, spread, out, held, data, lines, staged, sems, out_sems):
+def legendre_kernel(
+    waves, blocks, head, table, last_far, spread_far, out,
+    held, data, lines, staged, last, spread, sems, out_sems, side_sems,
+):
     lat, wide = table.shape[1:]
     pairs = last.shape[0]
     lanes = blocks.shape[2]
@@ -303,10 +314,17 @@
         pltpu.make_async_copy(table.at[pair], held.at[pair], sems.at[pair])
         for pair in range(pairs - HEAD)
     ]
-    for copy in copies:
+    for copy in copies[:1]:
+        copy.start()
+    sides = [
+        pltpu.make_async_copy(last_far, last, side_sems.at[0]),
+        pltpu.make_async_copy(spread_far, spread, side_sems.at[1]),
+    ]
+    for copy in sides + copies[1:]:
         copy.start()
     lane = lax.broadcasted_iota(jnp.int32, (4 * GROUP, lanes), 1)
-    for group in range(pairs // GROUP):
+
+    def prepare(group):
         for half in range(2):
             for field in range(4):
                 have = [
@@ -331,7 +349,10 @@
                                 half * lanes : (half + 1) * lanes,
                             ] = value[pair * 4 + kind * 2 : pair * 4 + kind * 2 + 2]
 
-    for pair in range(pairs):
+    for copy in sides:
+        copy.wait()
+
+    def edge(pair):
         wave = waves[pair]
         for side in range(2):
             value = jnp.sum(
@@ -350,9 +371,11 @@
     index = index[:16]
     parity, column = index & 1, index >> 1
     written = []
-    groups = [GROUP] * (pairs // GROUP - 1) + [GROUP // 2, GROUP // 4, GROUP // 4]
-    for group, count in enumerate(groups):
-        start = sum(groups[:group])
+    for group in range(pairs // GROUP):
+        start, count = group * GROUP, GROUP
+        prepare(group)
+        for pair in range(start, start + count):
+            edge(pair)
         for pair in range(start, start + count):
             if pair >= HEAD:
                 copies[pair - HEAD].wait()
@@ -403,8 +426,8 @@
             whole,
             whole,
             pl.BlockSpec(memory_space=pl.ANY),
-            whole,
-            whole,
+            pl.BlockSpec(memory_space=pl.ANY),
+            pl.BlockSpec(memory_space=pl.ANY),
         ],
         out_specs=pl.BlockSpec(memory_space=pl.ANY),
         scratch_shapes=[
@@ -412,8 +435,11 @@
             pltpu.VMEM((pairs, 2, 32, lat), jnp.float32),
             pltpu.VMEM((16 * pairs, wide), jnp.bfloat16),
             pltpu.VMEM((pairs, 2, 8, 2, columns), jnp.bfloat16),
+            pltpu.VMEM(last.shape, jnp.bfloat16),
+            pltpu.VMEM((256, 256), jnp.bfloat16),
             pltpu.SemaphoreType.DMA((pairs - HEAD,)),
-            pltpu.SemaphoreType.DMA((pairs // GROUP + 2,)),
+            pltpu.SemaphoreType.DMA((pairs // GROUP,)),
+            pltpu.SemaphoreType.DMA((2,)),
         ],
         out_shape=jax.ShapeDtypeStruct((pairs, 2, 8, 2, columns), jnp.bfloat16),
         compiler_params=pltpu.CompilerParams(vmem_limit_bytes=48 << 20),

time: 72 us -> 70.7 us (0.982)
  Pallas kernels: 38.3 us -> 36.9 us
    pallas_call x1, Pallas kernels: 11.2 us -> 10 us  [legendre_product(): pl.pallas_call(legendre_kernel, in_specs=[pl.BlockSpec(memory_space=pltpu...]
  transfers between devices with their start and end apart: 2 -> 2, of which waited for: 2 -> 2; matrix products, arithmetic and copies ran while one was open for 0% -> 0% of each run, Pallas kernels for 32% -> 33%
where the time goes in v5:
time: 70.7 us; the launch traced here: 70.3 us
  Pallas kernels  36.9 us (52%)
  waiting for transfers between devices  13.4 us (19%)
  starting transfers between devices  11.9 us (17%)
  local copies, waits for them, and re-layouts  8 us (11%)
    pallas_call x1, Pallas kernels, turned(): pl.pallas_call(turned_kernel, grid=(pairs,), in_specs=[pl.BlockSpec((1, c...  17.4 us
    all_to_all x1, waiting for transfers between devices, local(): got = lax.all_to_all(sent, AXES, 0, 0, tiled=True)  12.1 us
    pallas_call x1, Pallas kernels, legendre_product(): pl.pallas_call(legendre_kernel, in_specs=[pl.BlockSpec(memory_space=pltpu...  10 us
    unnamed x6, local copies, waits for them, and re-layouts  7.8 us
    all_to_all x1, starting transfers between devices, local(): waves = lax.all_to_all(repeated(slot_wave, devices), AXES, 0, 0, tiled=True)  7.3 us
    pallas_call x1, Pallas kernels, transform(): pl.pallas_call(transform_kernel, in_specs=[pl.BlockSpec(memory_space=pltp...  5.84 us
    all_to_all x1, starting transfers between devices, local(): got = lax.all_to_all(sent, AXES, 0, 0, tiled=True)  4.63 us
    pallas_call x1, Pallas kernels, ordered(): pl.pallas_call(order_kernel, in_specs=[whole, whole], out_specs=pl.BlockS...  2.45 us
  transfers between devices with their start and end apart: 2, of which 2 were waited for; matrix products, arithmetic and copies ran while one was open for 0% of the time, Pallas kernels for 33%

profile of v5, /device:TPU:0, one launch (start us, length us, event | category | flops | bytes accessed | tf_op | source)
XLA Modules:
  0.0 70.3 jit_solution(11777665887799931822)
XLA Ops:
  0.0 1.3 %repeated.1 = s32[32,1,32]{2,1,0:T(1,128)} custom-call(s32[1,1,32]{2,1,0:T(1,128)} %bitcast.3), custom_call_target="tpu_custom_call" | custom-call | tf_op jit(solution)/shard_map/repeated/pallas_call | solution.py:84
  1.3 7.3 %all-to-all-start = ((s32[32,1,32]{2,1,0:T(1,128)}), s32[32,1,32]{2,1,0:T(1,128)S(1)}, u32[]{:S(2)}, u32[]{:S(2)}) async-start(s32[32,1,32]{2,1,0:T(1,128)} %repeated.1), calls=%async_computation | async-start | bytes 32768 | tf_op jit(solution)/shard_map/all_to_all | solution.py:456
  8.6 5.8 %transform.1.fourier = bf16[4,512,384]{2,1,0:T(8,128)(2,1)S(1)} custom-call(s32[1]{0:T(128)} %bitcast.1.me, bf16[2,2,96,3072]{3,2,1,0:T(8,128)(2,1)} %grid.1, bf16[3,512,1536]{2,1,0:T(8,128)(2,1)} %constant.15.clone.table), custom_call_target="tpu_custom_call" | custom-call | flops 1811939328 | bytes 10485760 | tf_op jit(solution)/shard_map/transform/pallas_call | solution.py:163
  14.4 1.2 %all-to-all-done.waves = s32[32,1,32]{2,1,0:T(1,128)S(1)} async-done(((s32[32,1,32]{2,1,0:T(1,128)}), s32[32,1,32]{2,1,0:T(1,128)S(1)}, u32[]{:S(2)}, u32[]{:S(2)}) %all-to-all-start) | async-done | bytes 4128 | tf_op jit(solution)/shard_map/all_to_all | solution.py:456
  15.6 2.4 %ordered.1 = bf16[32,64,384]{2,1,0:T(8,128)(2,1)} custom-call(s32[32,1,32]{2,1,0:T(1,128)S(1)} %all-to-all-done.waves, bf16[4,512,384]{2,1,0:T(8,128)(2,1)S(1)} %transform.1.fourier), custom_call_target="tpu_custom_call" | custom-call | flops 805306368 | bytes 4194304 | tf_op jit(solution)/shard_map/ordered/pallas_call | solution.py:242
  18.1 0.0 copy-start.2
  18.1 4.6 %all-to-all-start.1 = ((bf16[32,64,384]{2,1,0:T(8,128)(2,1)}), bf16[32,64,384]{2,1,0:T(8,128)(2,1)S(1)}, u32[]{:S(2)}, u32[]{:S(2)}) async-start(bf16[32,64,384]{2,1,0:T(8,128)(2,1)} %ordered.1), calls=%async_computation.1 | async-start | bytes 3145728 | tf_op jit(solution)/shard_map/all_to_all | solution.py:460
  22.8 0.0 copy-done.2
  22.8 0.1 reshape.9
  22.8 0.1 slice_reduce_fusion.waves
  23.0 0.0 copy-start
  23.0 17.4 %turned.1 = (bf16[1,768,1024]{2,1,0:T(8,128)(2,1)S(1)}, bf16[15,768,1024]{2,1,0:T(8,128)(2,1)S(1)}, bf16[16,2,768]{2,1,0:T(2,128)(2,1)S(1)}) custom-call(bf16[16,513,2,768]{3,2,1,0:T(2,128)(2,1)} %bitcast.4), custom_call_target="tpu_custom_call" | custom-call | flops 21474836480 | bytes 62914560 | tf_op jit(solution)/shard_map/turned/pallas_call | solution.py:282
  40.3 0.0 copy-start.1
  40.4 7.8 %copy-done.1 = bf16[15,768,1024]{2,1,0:T(8,128)(2,1)} copy-done((bf16[15,768,1024]{2,1,0:T(8,128)(2,1)}, bf16[15,768,1024]{2,1,0:T(8,128)(2,1)S(1)}, u32[]{:S(2)}) %copy-start.1) | copy-done | bytes 23592984
  48.1 12.1 %all-to-all-done.1.blocks = bf16[32,64,384]{2,1,0:T(8,128)(2,1)S(1)} async-done(((bf16[32,64,384]{2,1,0:T(8,128)(2,1)}), bf16[32,64,384]{2,1,0:T(8,128)(2,1)S(1)}, u32[]{:S(2)}, u32[]{:S(2)}) %all-to-all-start.1) | async-done | bytes 1572896 | tf_op jit(solution)/shard_map/all_to_all | solution.py:460
  60.3 0.0 copy-done
  60.3 10.0 %legendre_product.1 = bf16[16,2,8,2,513]{4,3,2,1,0:T(2,128)(2,1)} custom-call(s32[16]{0:T(128)S(1)} %slice_reduce_fusion.waves, bf16[32,64,384]{2,1,0:T(8,128)(2,1)S(1)} %all-to-all-done.1.blocks, bf16[1,768,1024]{2,1,0:T(8,128)(2,1)S(1)} %get-tuple-element.8.head, bf16[15,768,1024]{2,1,0:T(8,128)(2,1)} %copy-done.1, ...), custom_call_target="tpu_custom_call" | custom-call | flops 8589934592 | bytes 31457280 | tf_op jit(solution)/shard_map/legendre_product/pallas_call | solution.py:422
Async XLA Ops:
  1.3 14.4 %all-to-all-start = ((s32[32,1,32]{2,1,0:T(1,128)}), s32[32,1,32]{2,1,0:T(1,128)S(1)}, u32[]{:S(2)}, u32[]{:S(2)}) async-start(s32[32,1,32]{2,1,0:T(1,128)} %repeated.1), calls=%async_computation | async-start | bytes 32768 | tf_op jit(solution)/shard_map/all_to_all | solution.py:456
  18.1 4.7 %copy-start.2 = (s32[32]{0:T(128)S(1)}, s32[32]{0:T(128)}, u32[]{:S(2)}) copy-start(s32[32]{0:T(128)} %param.7) | copy-start | bytes 388
  18.1 42.2 %all-to-all-start.1 = ((bf16[32,64,384]{2,1,0:T(8,128)(2,1)}), bf16[32,64,384]{2,1,0:T(8,128)(2,1)S(1)}, u32[]{:S(2)}, u32[]{:S(2)}) async-start(bf16[32,64,384]{2,1,0:T(8,128)(2,1)} %ordered.1), calls=%async_computation.1 | async-start | bytes 3145728 | tf_op jit(solution)/shard_map/all_to_all | solution.py:460
  23.0 37.3 %copy-start = (bf16[256,256]{1,0:T(8,128)(2,1)S(1)}, bf16[256,256]{1,0:T(8,128)(2,1)}, u32[]{:S(2)}) copy-start(bf16[256,256]{1,0:T(8,128)(2,1)} %constant.16.clone.spread_far) | copy-start | bytes 393220
  40.3 7.8 %copy-start.1 = (bf16[15,768,1024]{2,1,0:T(8,128)(2,1)}, bf16[15,768,1024]{2,1,0:T(8,128)(2,1)S(1)}, u32[]{:S(2)}) copy-start(bf16[15,768,1024]{2,1,0:T(8,128)(2,1)S(1)} %get-tuple-element.9.table) | copy-start | bytes 70778880

commit v6 on v5

--- a/solution.py
+++ b/solution.py
@@ -73,6 +73,7 @@
 NT = (((1,), (1,)), ((), ()))
 GROUP = 4
 HEAD = 1
+PARTS = ((0, 12), (12, 12), (24, 8))
 
 
 def repeat_kernel(wave, out):
@@ -202,14 +203,12 @@
     square[...] = square[...].T
     number = quarter_order(lax.broadcasted_iota(jnp.int32, (pairs, count), 1))
     firsts = square[pl.ds(0, pairs, stride=2), :]
-    for device in range(devices):
-        wave = firsts[:, device : device + 1]
-        picks[device * pairs : (device + 1) * pairs, :] = (
-            jnp.where(wave == number, 1.0, 0.0).astype(jnp.bfloat16)
-        )
     copies = []
-    share = 8
-    for first in range(0, devices, share):
+    for part, (first, share) in enumerate(PARTS):
+        for device in range(first, first + share):
+            picks[device * pairs : (device + 1) * pairs, :] = (
+                jnp.where(firsts[:, device : device + 1] == number, 1.0, 0.0).astype(jnp.bfloat16)
+            )
         for kind in range(kinds):
             got = jnp.dot(
                 picks[first * pairs : (first + share) * pairs, :],
@@ -225,10 +224,8 @@
                 staged[device, :, tile * 128 : tile * 128 + 128] = rows_f32[
                     tile, device * size : (device + 1) * size, :
                 ].astype(jnp.bfloat16)
-        part = pl.ds(first, share)
-        copies.append(
-            pltpu.make_async_copy(staged.at[part], out.at[part], sems.at[first // share])
-        )
+        rows = pl.ds(first, share)
+        copies.append(pltpu.make_async_copy(staged.at[rows], out.at[rows], sems.at[part]))
         copies[-1].start()
     for copy in copies:
         copy.wait()
@@ -248,7 +245,7 @@
             pltpu.VMEM((slots, count), jnp.bfloat16),
             pltpu.VMEM((lanes // 128, kinds * slots, 128), jnp.float32),
             pltpu.VMEM((devices, kinds * pairs, lanes), jnp.bfloat16),
-            pltpu.SemaphoreType.DMA((devices // 8,)),
+            pltpu.SemaphoreType.DMA((len(PARTS),)),
         ],
         out_shape=jax.ShapeDtypeStruct((devices, kinds * pairs, lanes), jnp.bfloat16),
         compiler_params=pltpu.CompilerParams(vmem_limit_bytes=24 << 20),

time: 70.7 us -> 70.7 us (level)
  no operation moved by 1% of the time
where the time goes in v6:
time: 70.7 us; the launch traced here: 70.3 us
  Pallas kernels  36.9 us (52%)
  waiting for transfers between devices  13.4 us (19%)
  starting transfers between devices  11.9 us (17%)
  local copies, waits for them, and re-layouts  8 us (11%)
    pallas_call x1, Pallas kernels, turned(): pl.pallas_call(turned_kernel, grid=(pairs,), in_specs=[pl.BlockSpec((1, c...  17.4 us
    all_to_all x1, waiting for transfers between devices, local(): got = lax.all_to_all(sent, AXES, 0, 0, tiled=True)  12.1 us
    pallas_call x1, Pallas kernels, legendre_product(): pl.pallas_call(legendre_kernel, in_specs=[pl.BlockSpec(memory_space=pltpu...  10 us
    unnamed x6, local copies, waits for them, and re-layouts  7.8 us
    all_to_all x1, starting transfers between devices, local(): waves = lax.all_to_all(repeated(slot_wave, devices), AXES, 0, 0, tiled=True)  7.3 us
    pallas_call x1, Pallas kernels, transform(): pl.pallas_call(transform_kernel, in_specs=[pl.BlockSpec(memory_space=pltp...  5.84 us
    all_to_all x1, starting transfers between devices, local(): got = lax.all_to_all(sent, AXES, 0, 0, tiled=True)  4.62 us
    pallas_call x1, Pallas kernels, ordered(): pl.pallas_call(order_kernel, in_specs=[whole, whole], out_specs=pl.BlockS...  2.42 us
  transfers between devices with their start and end apart: 2, of which 2 were waited for; matrix products, arithmetic and copies ran while one was open for 0% of the time, Pallas kernels for 33%

profile of v6, /device:TPU:0, one launch (start us, length us, event | category | flops | bytes accessed | tf_op | source)
XLA Modules:
  0.0 70.3 jit_solution(7181733579345082960)
XLA Ops:
  0.0 1.3 %repeated.1 = s32[32,1,32]{2,1,0:T(1,128)} custom-call(s32[1,1,32]{2,1,0:T(1,128)} %bitcast.3), custom_call_target="tpu_custom_call" | custom-call | tf_op jit(solution)/shard_map/repeated/pallas_call | solution.py:85
  1.3 7.3 %all-to-all-start = ((s32[32,1,32]{2,1,0:T(1,128)}), s32[32,1,32]{2,1,0:T(1,128)S(1)}, u32[]{:S(2)}, u32[]{:S(2)}) async-start(s32[32,1,32]{2,1,0:T(1,128)} %repeated.1), calls=%async_computation | async-start | bytes 32768 | tf_op jit(solution)/shard_map/all_to_all | solution.py:453
  8.6 5.8 %transform.1.fourier = bf16[4,512,384]{2,1,0:T(8,128)(2,1)S(1)} custom-call(s32[1]{0:T(128)} %bitcast.1.me, bf16[2,2,96,3072]{3,2,1,0:T(8,128)(2,1)} %grid.1, bf16[3,512,1536]{2,1,0:T(8,128)(2,1)} %constant.15.clone.table), custom_call_target="tpu_custom_call" | custom-call | flops 1811939328 | bytes 10485760 | tf_op jit(solution)/shard_map/transform/pallas_call | solution.py:164
  14.4 1.2 %all-to-all-done.waves = s32[32,1,32]{2,1,0:T(1,128)S(1)} async-done(((s32[32,1,32]{2,1,0:T(1,128)}), s32[32,1,32]{2,1,0:T(1,128)S(1)}, u32[]{:S(2)}, u32[]{:S(2)}) %all-to-all-start) | async-done | bytes 4128 | tf_op jit(solution)/shard_map/all_to_all | solution.py:453
  15.6 2.4 %ordered.1 = bf16[32,64,384]{2,1,0:T(8,128)(2,1)} custom-call(s32[32,1,32]{2,1,0:T(1,128)S(1)} %all-to-all-done.waves, bf16[4,512,384]{2,1,0:T(8,128)(2,1)S(1)} %transform.1.fourier), custom_call_target="tpu_custom_call" | custom-call | flops 805306368 | bytes 4194304 | tf_op jit(solution)/shard_map/ordered/pallas_call | solution.py:239
  18.1 0.0 copy-start.2
  18.1 4.6 %all-to-all-start.1 = ((bf16[32,64,384]{2,1,0:T(8,128)(2,1)}), bf16[32,64,384]{2,1,0:T(8,128)(2,1)S(1)}, u32[]{:S(2)}, u32[]{:S(2)}) async-start(bf16[32,64,384]{2,1,0:T(8,128)(2,1)} %ordered.1), calls=%async_computation.1 | async-start | bytes 3145728 | tf_op jit(solution)/shard_map/all_to_all | solution.py:457
  22.7 0.0 copy-done.2
  22.7 0.1 reshape.9
  22.8 0.1 slice_reduce_fusion.waves
  22.9 0.0 copy-start
  22.9 17.4 %turned.1 = (bf16[1,768,1024]{2,1,0:T(8,128)(2,1)S(1)}, bf16[15,768,1024]{2,1,0:T(8,128)(2,1)S(1)}, bf16[16,2,768]{2,1,0:T(2,128)(2,1)S(1)}) custom-call(bf16[16,513,2,768]{3,2,1,0:T(2,128)(2,1)} %bitcast.4), custom_call_target="tpu_custom_call" | custom-call | flops 21474836480 | bytes 62914560 | tf_op jit(solution)/shard_map/turned/pallas_call | solution.py:279
  40.3 0.0 copy-start.1
  40.3 7.8 %copy-done.1 = bf16[15,768,1024]{2,1,0:T(8,128)(2,1)} copy-done((bf16[15,768,1024]{2,1,0:T(8,128)(2,1)}, bf16[15,768,1024]{2,1,0:T(8,128)(2,1)S(1)}, u32[]{:S(2)}) %copy-start.1) | copy-done | bytes 23592984
  48.1 12.1 %all-to-all-done.1.blocks = bf16[32,64,384]{2,1,0:T(8,128)(2,1)S(1)} async-done(((bf16[32,64,384]{2,1,0:T(8,128)(2,1)}), bf16[32,64,384]{2,1,0:T(8,128)(2,1)S(1)}, u32[]{:S(2)}, u32[]{:S(2)}) %all-to-all-start.1) | async-done | bytes 1572896 | tf_op jit(solution)/shard_map/all_to_all | solution.py:457
  60.2 0.0 copy-done
  60.2 10.0 %legendre_product.1 = bf16[16,2,8,2,513]{4,3,2,1,0:T(2,128)(2,1)} custom-call(s32[16]{0:T(128)S(1)} %slice_reduce_fusion.waves, bf16[32,64,384]{2,1,0:T(8,128)(2,1)S(1)} %all-to-all-done.1.blocks, bf16[1,768,1024]{2,1,0:T(8,128)(2,1)S(1)} %get-tuple-element.8.head, bf16[15,768,1024]{2,1,0:T(8,128)(2,1)} %copy-done.1, ...), custom_call_target="tpu_custom_call" | custom-call | flops 8589934592 | bytes 31457280 | tf_op jit(solution)/shard_map/legendre_product/pallas_call | solution.py:419
Async XLA Ops:
  1.3 14.4 %all-to-all-start = ((s32[32,1,32]{2,1,0:T(1,128)}), s32[32,1,32]{2,1,0:T(1,128)S(1)}, u32[]{:S(2)}, u32[]{:S(2)}) async-start(s32[32,1,32]{2,1,0:T(1,128)} %repeated.1), calls=%async_computation | async-start | bytes 32768 | tf_op jit(solution)/shard_map/all_to_all | solution.py:453
  18.1 4.6 %copy-start.2 = (s32[32]{0:T(128)S(1)}, s32[32]{0:T(128)}, u32[]{:S(2)}) copy-start(s32[32]{0:T(128)} %param.7) | copy-start | bytes 388
  18.1 42.1 %all-to-all-start.1 = ((bf16[32,64,384]{2,1,0:T(8,128)(2,1)}), bf16[32,64,384]{2,1,0:T(8,128)(2,1)S(1)}, u32[]{:S(2)}, u32[]{:S(2)}) async-start(bf16[32,64,384]{2,1,0:T(8,128)(2,1)} %ordered.1), calls=%async_computation.1 | async-start | bytes 3145728 | tf_op jit(solution)/shard_map/all_to_all | solution.py:457
  22.9 37.3 %copy-start = (bf16[256,256]{1,0:T(8,128)(2,1)S(1)}, bf16[256,256]{1,0:T(8,128)(2,1)}, u32[]{:S(2)}) copy-start(bf16[256,256]{1,0:T(8,128)(2,1)} %constant.16.clone.spread_far) | copy-start | bytes 393220
  40.3 7.8 %copy-start.1 = (bf16[15,768,1024]{2,1,0:T(8,128)(2,1)}, bf16[15,768,1024]{2,1,0:T(8,128)(2,1)S(1)}, u32[]{:S(2)}) copy-start(bf16[15,768,1024]{2,1,0:T(8,128)(2,1)S(1)} %get-tuple-element.9.table) | copy-start | bytes 70778880

commit v7 on v6

--- a/solution.py
+++ b/solution.py
@@ -370,10 +370,13 @@
     written = []
     for group in range(pairs // GROUP):
         start, count = group * GROUP, GROUP
-        prepare(group)
+        if group == 0:
+            prepare(0)
         for pair in range(start, start + count):
             edge(pair)
         for pair in range(start, start + count):
+            if pair == start + count - 1 and start + count < pairs:
+                prepare(group + 1)
             if pair >= HEAD:
                 copies[pair - HEAD].wait()
             matrix = head[pair] if pair < HEAD else held[pair - HEAD]

time: 70.7 us -> 70.5 us (level)
  no operation moved by 1% of the time
where the time goes in v7:
time: 70.5 us; the launch traced here: 70.1 us
  Pallas kernels  36.8 us (52%)
  waiting for transfers between devices  13.4 us (19%)
  starting transfers between devices  11.9 us (17%)
  local copies, waits for them, and re-layouts  8 us (11%)
    pallas_call x1, Pallas kernels, turned(): pl.pallas_call(turned_kernel, grid=(pairs,), in_specs=[pl.BlockSpec((1, c...  17.4 us
    all_to_all x1, waiting for transfers between devices, local(): got = lax.all_to_all(sent, AXES, 0, 0, tiled=True)  12.1 us
    pallas_call x1, Pallas kernels, legendre_product(): pl.pallas_call(legendre_kernel, in_specs=[pl.BlockSpec(memory_space=pltpu...  9.91 us
    unnamed x6, local copies, waits for them, and re-layouts  7.8 us
    all_to_all x1, starting transfers between devices, local(): waves = lax.all_to_all(repeated(slot_wave, devices), AXES, 0, 0, tiled=True)  7.3 us
    pallas_call x1, Pallas kernels, transform(): pl.pallas_call(transform_kernel, in_specs=[pl.BlockSpec(memory_space=pltp...  5.84 us
    all_to_all x1, starting transfers between devices, local(): got = lax.all_to_all(sent, AXES, 0, 0, tiled=True)  4.62 us
    pallas_call x1, Pallas kernels, ordered(): pl.pallas_call(order_kernel, in_specs=[whole, whole], out_specs=pl.BlockS...  2.42 us
  transfers between devices with their start and end apart: 2, of which 2 were waited for; matrix products, arithmetic and copies ran while one was open for 0% of the time, Pallas kernels for 33%

profile of v7, /device:TPU:0, one launch (start us, length us, event | category | flops | bytes accessed | tf_op | source)
XLA Modules:
  0.0 70.1 jit_solution(8862811888913139217)
XLA Ops:
  0.0 1.3 %repeated.1 = s32[32,1,32]{2,1,0:T(1,128)} custom-call(s32[1,1,32]{2,1,0:T(1,128)} %bitcast.3), custom_call_target="tpu_custom_call" | custom-call | tf_op jit(solution)/shard_map/repeated/pallas_call | solution.py:85
  1.3 7.3 %all-to-all-start = ((s32[32,1,32]{2,1,0:T(1,128)}), s32[32,1,32]{2,1,0:T(1,128)S(1)}, u32[]{:S(2)}, u32[]{:S(2)}) async-start(s32[32,1,32]{2,1,0:T(1,128)} %repeated.1), calls=%async_computation | async-start | bytes 32768 | tf_op jit(solution)/shard_map/all_to_all | solution.py:456
  8.6 5.8 %transform.1.fourier = bf16[4,512,384]{2,1,0:T(8,128)(2,1)S(1)} custom-call(s32[1]{0:T(128)} %bitcast.1.me, bf16[2,2,96,3072]{3,2,1,0:T(8,128)(2,1)} %grid.1, bf16[3,512,1536]{2,1,0:T(8,128)(2,1)} %constant.15.clone.table), custom_call_target="tpu_custom_call" | custom-call | flops 1811939328 | bytes 10485760 | tf_op jit(solution)/shard_map/transform/pallas_call | solution.py:164
  14.4 1.2 %all-to-all-done.waves = s32[32,1,32]{2,1,0:T(1,128)S(1)} async-done(((s32[32,1,32]{2,1,0:T(1,128)}), s32[32,1,32]{2,1,0:T(1,128)S(1)}, u32[]{:S(2)}, u32[]{:S(2)}) %all-to-all-start) | async-done | bytes 4128 | tf_op jit(solution)/shard_map/all_to_all | solution.py:456
  15.6 2.4 %ordered.1 = bf16[32,64,384]{2,1,0:T(8,128)(2,1)} custom-call(s32[32,1,32]{2,1,0:T(1,128)S(1)} %all-to-all-done.waves, bf16[4,512,384]{2,1,0:T(8,128)(2,1)S(1)} %transform.1.fourier), custom_call_target="tpu_custom_call" | custom-call | flops 805306368 | bytes 4194304 | tf_op jit(solution)/shard_map/ordered/pallas_call | solution.py:239
  18.1 0.0 copy-start.2
  18.1 4.6 %all-to-all-start.1 = ((bf16[32,64,384]{2,1,0:T(8,128)(2,1)}), bf16[32,64,384]{2,1,0:T(8,128)(2,1)S(1)}, u32[]{:S(2)}, u32[]{:S(2)}) async-start(bf16[32,64,384]{2,1,0:T(8,128)(2,1)} %ordered.1), calls=%async_computation.1 | async-start | bytes 3145728 | tf_op jit(solution)/shard_map/all_to_all | solution.py:460
  22.7 0.0 copy-done.2
  22.7 0.1 reshape.9
  22.8 0.1 slice_reduce_fusion.waves
  22.9 0.0 copy-start
  22.9 17.4 %turned.1 = (bf16[1,768,1024]{2,1,0:T(8,128)(2,1)S(1)}, bf16[15,768,1024]{2,1,0:T(8,128)(2,1)S(1)}, bf16[16,2,768]{2,1,0:T(2,128)(2,1)S(1)}) custom-call(bf16[16,513,2,768]{3,2,1,0:T(2,128)(2,1)} %bitcast.4), custom_call_target="tpu_custom_call" | custom-call | flops 21474836480 | bytes 62914560 | tf_op jit(solution)/shard_map/turned/pallas_call | solution.py:279
  40.3 0.0 copy-start.1
  40.3 7.8 %copy-done.1 = bf16[15,768,1024]{2,1,0:T(8,128)(2,1)} copy-done((bf16[15,768,1024]{2,1,0:T(8,128)(2,1)}, bf16[15,768,1024]{2,1,0:T(8,128)(2,1)S(1)}, u32[]{:S(2)}) %copy-start.1) | copy-done | bytes 23592984
  48.1 12.1 %all-to-all-done.1.blocks = bf16[32,64,384]{2,1,0:T(8,128)(2,1)S(1)} async-done(((bf16[32,64,384]{2,1,0:T(8,128)(2,1)}), bf16[32,64,384]{2,1,0:T(8,128)(2,1)S(1)}, u32[]{:S(2)}, u32[]{:S(2)}) %all-to-all-start.1) | async-done | bytes 1572896 | tf_op jit(solution)/shard_map/all_to_all | solution.py:460
  60.2 0.0 copy-done
  60.2 9.9 %legendre_product.1 = bf16[16,2,8,2,513]{4,3,2,1,0:T(2,128)(2,1)} custom-call(s32[16]{0:T(128)S(1)} %slice_reduce_fusion.waves, bf16[32,64,384]{2,1,0:T(8,128)(2,1)S(1)} %all-to-all-done.1.blocks, bf16[1,768,1024]{2,1,0:T(8,128)(2,1)S(1)} %get-tuple-element.8.head, bf16[15,768,1024]{2,1,0:T(8,128)(2,1)} %copy-done.1, ...), custom_call_target="tpu_custom_call" | custom-call | flops 8589934592 | bytes 31457280 | tf_op jit(solution)/shard_map/legendre_product/pallas_call | solution.py:422
Async XLA Ops:
  1.3 14.4 %all-to-all-start = ((s32[32,1,32]{2,1,0:T(1,128)}), s32[32,1,32]{2,1,0:T(1,128)S(1)}, u32[]{:S(2)}, u32[]{:S(2)}) async-start(s32[32,1,32]{2,1,0:T(1,128)} %repeated.1), calls=%async_computation | async-start | bytes 32768 | tf_op jit(solution)/shard_map/all_to_all | solution.py:456
  18.1 4.6 %copy-start.2 = (s32[32]{0:T(128)S(1)}, s32[32]{0:T(128)}, u32[]{:S(2)}) copy-start(s32[32]{0:T(128)} %param.7) | copy-start | bytes 388
  18.1 42.1 %all-to-all-start.1 = ((bf16[32,64,384]{2,1,0:T(8,128)(2,1)}), bf16[32,64,384]{2,1,0:T(8,128)(2,1)S(1)}, u32[]{:S(2)}, u32[]{:S(2)}) async-start(bf16[32,64,384]{2,1,0:T(8,128)(2,1)} %ordered.1), calls=%async_computation.1 | async-start | bytes 3145728 | tf_op jit(solution)/shard_map/all_to_all | solution.py:460
  22.9 37.3 %copy-start = (bf16[256,256]{1,0:T(8,128)(2,1)S(1)}, bf16[256,256]{1,0:T(8,128)(2,1)}, u32[]{:S(2)}) copy-start(bf16[256,256]{1,0:T(8,128)(2,1)} %constant.16.clone.spread_far) | copy-start | bytes 393220
  40.3 7.8 %copy-start.1 = (bf16[15,768,1024]{2,1,0:T(8,128)(2,1)}, bf16[15,768,1024]{2,1,0:T(8,128)(2,1)S(1)}, u32[]{:S(2)}) copy-start(bf16[15,768,1024]{2,1,0:T(8,128)(2,1)S(1)} %get-tuple-element.9.table) | copy-start | bytes 70778880
